TPU v7x, 512 devices: a whole 4x4x16 slice. The times are simulated.
512 devices in a mesh: ctx: 32 (over x_lo, z), mp: 16 (over y, x_hi, core).
Axes of the slice: x: 4 (x_hi: 2, x_lo: 2; x = x_hi * 2 + x_lo), y: 4, z: 16, core: 2. Of those that a mesh axis runs over, the one named last changes fastest.
Arguments:
- values: bfloat16 [8192, 4096], P('ctx', 'mp'), may hold values from -6 to 6
- gates: bfloat16 [8192, 4096], P('ctx', 'mp'), may hold values from -6 to 6
- cotangent: bfloat16 [8192, 4096], P('ctx', 'mp'), may hold values from -6 to 6
- filters: bfloat16 [8192, 256], P('ctx', 'mp'), may hold values from -6 to 6
- skip_gain: float32 [4096], P('mp'), may hold values from -4 to 4
Outputs:
- grad_gates: bfloat16 [8192, 4096], P('ctx', 'mp')
- grad_values: bfloat16 [8192, 4096], P('ctx', 'mp')
- grad_filters: bfloat16 [8192, 256], P('ctx', 'mp')
All inputs are finite; a program needn't handle non-finite values.
Results may differ from a plain program's by a relative error of at most 0.022.
Values may be sent and summed in bfloat16 or wider, within the bound.
No kernel may reach another device: no remote copies, remote signals or barrier semaphores. Data moves between devices by JAX's collectives and lax.ppermute only.
A program may use at most 64 MiB of HBM per device.

v0:
```python
import math

import jax
import jax.numpy as jnp
from jax import lax
from jax.sharding import PartitionSpec as P


def angle_table(height, breadth, period):
    row_index = lax.broadcasted_iota(jnp.int32, (height, breadth), 0)
    col_index = lax.broadcasted_iota(jnp.int32, (height, breadth), 1)
    phases = (row_index * col_index % period).astype(jnp.float32) * (2.0 * math.pi / period)
    return (jnp.cos(phases), jnp.sin(phases))


def spread_columns(columns, offset, points):
    sources = columns.shape[0]
    block_rows = columns.shape[1]
    cos_outer, sin_outer = angle_table(2 * sources, sources, 2 * sources)
    real_part = jnp.einsum("ka,abc->kbc", cos_outer, columns, precision=lax.Precision.HIGHEST)
    imag_part = -jnp.einsum("ka,abc->kbc", sin_outer, columns, precision=lax.Precision.HIGHEST)
    freq_index = lax.broadcasted_iota(jnp.int32, (2 * sources, block_rows), 0)
    row_index = offset + lax.broadcasted_iota(jnp.int32, (2 * sources, block_rows), 1)
    phases = (freq_index * row_index % points).astype(jnp.float32) * (2.0 * math.pi / points)
    cos_twist = jnp.cos(phases)[:, :, None]
    sin_twist = jnp.sin(phases)[:, :, None]
    return jnp.stack(
        [
            real_part * cos_twist + imag_part * sin_twist,
            imag_part * cos_twist - real_part * sin_twist,
        ]
    )


def finish_forward(partial_value):
    rows_all = partial_value.shape[2]
    cos_inner, sin_inner = angle_table(rows_all, rows_all, rows_all)
    cos_terms = jnp.einsum(
        "skbc,bm->skmc", partial_value, cos_inner, precision=lax.Precision.HIGHEST
    )
    sin_terms = jnp.einsum(
        "skbc,bm->skmc", partial_value, sin_inner, precision=lax.Precision.HIGHEST
    )
    return jnp.stack([cos_terms[0] + sin_terms[1], cos_terms[1] - sin_terms[0]])


def start_inverse(spectrum, first_freq, points):
    rows_all = spectrum.shape[2]
    freq_count = spectrum.shape[1]
    cos_inner, sin_inner = angle_table(rows_all, rows_all, rows_all)
    cos_terms = jnp.einsum("skmc,mb->skbc", spectrum, cos_inner, precision=lax.Precision.HIGHEST)
    sin_terms = jnp.einsum("skmc,mb->skbc", spectrum, sin_inner, precision=lax.Precision.HIGHEST)
    real_part = cos_terms[0] - sin_terms[1]
    imag_part = cos_terms[1] + sin_terms[0]
    freq_index = first_freq + lax.broadcasted_iota(jnp.int32, (freq_count, rows_all), 0)
    row_index = lax.broadcasted_iota(jnp.int32, (freq_count, rows_all), 1)
    phases = (freq_index * row_index % points).astype(jnp.float32) * (2.0 * math.pi / points)
    cos_twist = jnp.cos(phases)[:, :, None]
    sin_twist = jnp.sin(phases)[:, :, None]
    return jnp.stack(
        [
            real_part * cos_twist - imag_part * sin_twist,
            imag_part * cos_twist + real_part * sin_twist,
        ]
    )


def finish_inverse(gathered, points):
    freqs = gathered.shape[1]
    cos_outer, sin_outer = angle_table(freqs, freqs // 2, freqs)
    result = jnp.einsum("kbc,ka->abc", gathered[0], cos_outer, precision=lax.Precision.HIGHEST)
    result = result - jnp.einsum(
        "kbc,ka->abc", gathered[1], sin_outer, precision=lax.Precision.HIGHEST
    )
    return result * (1.0 / points)


def spectral_products(filter_spec, value_spec, gated_spec):
    filt_real, filt_imag = (filter_spec[0], filter_spec[1])
    value_real, value_imag = (value_spec[0], value_spec[1])
    gated_real, gated_imag = (gated_spec[0], gated_spec[1])
    conv_spec = jnp.stack(
        [
            filt_real * value_real - filt_imag * value_imag,
            filt_real * value_imag + filt_imag * value_real,
        ]
    )
    back_spec = jnp.stack(
        [
            filt_real * gated_real + filt_imag * gated_imag,
            filt_real * gated_imag - filt_imag * gated_real,
        ]
    )
    lag_spec = jnp.stack(
        [
            gated_real * value_real + gated_imag * value_imag,
            gated_imag * value_real - gated_real * value_imag,
        ]
    )
    return (conv_spec, back_spec, lag_spec)


def forward_three(paired, filter_block, ctx_place, points):
    paired_cols, filter_cols = (
        lax.all_to_all(paired, "ctx", split_axis=2, concat_axis=1, tiled=True),
        lax.all_to_all(filter_block, "ctx", split_axis=2, concat_axis=1, tiled=True),
    )
    block_rows = paired_cols.shape[2]
    offset = ctx_place * block_rows
    value_part = spread_columns(paired_cols[0].astype(jnp.float32), offset, points)
    gated_part = spread_columns(paired_cols[1].astype(jnp.float32), offset, points)
    filter_part = spread_columns(filter_cols[0].astype(jnp.float32), offset, points)
    value_part, gated_part, filter_part = (
        lax.all_to_all(
            value_part.astype(jnp.bfloat16), "ctx", split_axis=1, concat_axis=2, tiled=True
        ).astype(value_part.dtype),
        lax.all_to_all(
            gated_part.astype(jnp.bfloat16), "ctx", split_axis=1, concat_axis=2, tiled=True
        ).astype(gated_part.dtype),
        lax.all_to_all(
            filter_part.astype(jnp.bfloat16), "ctx", split_axis=1, concat_axis=2, tiled=True
        ).astype(filter_part.dtype),
    )
    return (finish_forward(value_part), finish_forward(gated_part), finish_forward(filter_part))


def inverse_three(conv_spec, back_spec, lag_spec, ctx_place, points):
    first_freq = conv_spec.shape[1] * ctx_place
    conv_part = start_inverse(conv_spec, first_freq, points)
    back_part = start_inverse(back_spec, first_freq, points)
    lag_part = start_inverse(lag_spec, first_freq, points)
    conv_part, back_part, lag_part = (
        lax.all_to_all(
            conv_part.astype(jnp.bfloat16), "ctx", split_axis=2, concat_axis=1, tiled=True
        ).astype(conv_part.dtype),
        lax.all_to_all(
            back_part.astype(jnp.bfloat16), "ctx", split_axis=2, concat_axis=1, tiled=True
        ).astype(back_part.dtype),
        lax.all_to_all(
            lag_part.astype(jnp.bfloat16), "ctx", split_axis=2, concat_axis=1, tiled=True
        ).astype(lag_part.dtype),
    )
    conv_part = finish_inverse(conv_part, points)
    back_part = finish_inverse(back_part, points)
    lag_part = finish_inverse(lag_part, points)
    conv_part, back_part, lag_part = (
        lax.all_to_all(
            conv_part.astype(jnp.bfloat16), "ctx", split_axis=0, concat_axis=1, tiled=True
        ).astype(conv_part.dtype),
        lax.all_to_all(
            back_part.astype(jnp.bfloat16), "ctx", split_axis=0, concat_axis=1, tiled=True
        ).astype(back_part.dtype),
        lax.all_to_all(
            lag_part.astype(jnp.bfloat16), "ctx", split_axis=0, concat_axis=1, tiled=True
        ).astype(lag_part.dtype),
    )
    return (conv_part[0], back_part[0], lag_part[0])


def per_device(values, gates, cotangent, filters, skip_gain):
    ctx_size = lax.axis_size("ctx")
    ctx_place = lax.axis_index("ctx")
    length = values.shape[0]
    points = 2 * ctx_size * length
    factor = 1.0 / math.sqrt(ctx_size * length)
    cot_f = cotangent.astype(jnp.float32)
    gated = (cot_f * gates.astype(jnp.float32)).astype(jnp.bfloat16)
    paired = jnp.stack([values, gated])[:, None]
    all_filters = lax.all_gather(filters, "mp", axis=1, tiled=True)
    value_spec, gated_spec, filter_spec = forward_three(
        paired, all_filters[None, None], ctx_place, points
    )
    filter_spec = filter_spec * factor
    conv_spec, back_spec, lag_spec = spectral_products(filter_spec, value_spec, gated_spec)
    conv, back, lagged = inverse_three(conv_spec, back_spec, lag_spec, ctx_place, points)
    grad_filters = lax.psum_scatter(
        (lagged * factor).astype(jnp.bfloat16), "mp", scatter_dimension=1, tiled=True
    )
    skip_row = skip_gain[None, :]
    value_f = values.astype(jnp.float32)
    gated_f = gated.astype(jnp.float32)
    grad_gates = (cot_f * (conv + skip_row * value_f)).astype(jnp.bfloat16)
    grad_values = (back + skip_row * gated_f).astype(jnp.bfloat16)
    return (grad_gates, grad_values, grad_filters)


def solution(mesh):
    return jax.shard_map(
        per_device,
        mesh=mesh,
        in_specs=(P("ctx", "mp"), P("ctx", "mp"), P("ctx", "mp"), P("ctx", "mp"), P("mp")),
        out_specs=(P("ctx", "mp"), P("ctx", "mp"), P("ctx", "mp")),
        check_vma=False,
    )
```

profile of v0, /device:TPU:1, one launch (start us, length us, event | category | flops | bytes accessed | tf_op | source)
XLA Modules:
  0.0 463.1 jit_solution(10448787724557526549)
XLA Ops:
  7.2 26.5 %all_gather.3 = bf16[256,256]{0,1:T(8,128)(2,1)S(1)} all-gather(bf16[256,16]{0,1:T(8,128)(2,1)} %param.8), channel_id=1, replica_groups=mesh['ctx'=32,'mp'=16] {'mp'}, dimensions={1}, use_global_device_ids=true | all-gather | bytes 139264 | tf_op jit(solution)/shard_map/all_gather | solution.py:169
  36.5 15.4 %all-to-all-start = ((bf16[32,2,1024]{2,1,0:T(2,128)(2,1)}), bf16[32,2,1024]{2,1,0:T(2,128)(2,1)S(1)}, u32[]{:S(2)}, u32[]{:S(2)}) async-start(bf16[32,2,1024]{2,1,0:T(2,128)(2,1)} %reshape.155), calls=%async_computation | async-start | bytes 262144 | tf_op jit(solution)/shard_map/all_to_all | solution.py:106
  53.8 13.3 %all-to-all-done = bf16[32,2,1024]{2,1,0:T(2,128)(2,1)S(1)} async-done(((bf16[32,2,1024]{2,1,0:T(2,128)(2,1)}), bf16[32,2,1024]{2,1,0:T(2,128)(2,1)S(1)}, u32[]{:S(2)}, u32[]{:S(2)}) %all-to-all-start) | async-done | bytes 131104 | tf_op jit(solution)/shard_map/all_to_all | solution.py:106
  67.1 4.2 all-to-all-start.2
  72.0 17.3 %all-to-all-done.2 = bf16[2,1,256,256]{3,0,1,2:T(2,128)(2,1)S(1)} async-done(((bf16[2,1,256,256]{3,0,1,2:T(2,128)(2,1)}), bf16[2,1,256,256]{3,0,1,2:T(2,128)(2,1)S(1)}, u32[]{:S(2)}, u32[]{:S(2)}) %all-to-all-start.2) | async-done | bytes 262176 | tf_op jit(solution)/shard_map/all_to_all | solution.py:105
  93.6 6.0 %all-to-all-start.3 = ((bf16[2,64,8,256]{3,2,0,1:T(8,128)(2,1)}), bf16[2,64,8,256]{3,2,0,1:T(8,128)(2,1)S(1)}, u32[]{:S(2)}, u32[]{:S(2)}) async-start(bf16[2,64,8,256]{3,2,0,1:T(8,128)(2,1)} %copy.72), calls=%async_computation.3 | async-start | bytes 1048576 | tf_op jit(solution)/shard_map/all_to_all | solution.py:114
  100.8 26.4 %all-to-all-done.3 = bf16[2,64,8,256]{3,2,0,1:T(8,128)(2,1)S(1)} async-done(((bf16[2,64,8,256]{3,2,0,1:T(8,128)(2,1)}), bf16[2,64,8,256]{3,2,0,1:T(8,128)(2,1)S(1)}, u32[]{:S(2)}, u32[]{:S(2)}) %all-to-all-start.3) | async-done | bytes 524320 | tf_op jit(solution)/shard_map/all_to_all | solution.py:114
  127.2 7.5 %all-to-all-start.6 = ((bf16[2,64,8,256]{3,2,0,1:T(8,128)(2,1)}), bf16[2,64,8,256]{3,2,0,1:T(8,128)(2,1)S(1)}, u32[]{:S(2)}, u32[]{:S(2)}) async-start(bf16[2,64,8,256]{3,2,0,1:T(8,128)(2,1)} %copy.80), calls=%async_computation.6 | async-start | bytes 1048576 | tf_op jit(solution)/shard_map/all_to_all | solution.py:117
  135.9 27.1 %all-to-all-done.6 = bf16[2,64,8,256]{3,2,0,1:T(8,128)(2,1)S(1)} async-done(((bf16[2,64,8,256]{3,2,0,1:T(8,128)(2,1)}), bf16[2,64,8,256]{3,2,0,1:T(8,128)(2,1)S(1)}, u32[]{:S(2)}, u32[]{:S(2)}) %all-to-all-start.6) | async-done | bytes 524320 | tf_op jit(solution)/shard_map/all_to_all | solution.py:117
  163.0 7.5 %all-to-all-start.1 = ((bf16[2,64,8,256]{3,2,0,1:T(8,128)(2,1)}), bf16[2,64,8,256]{3,2,0,1:T(8,128)(2,1)}, u32[]{:S(2)}, u32[]{:S(2)}) async-start(bf16[2,64,8,256]{3,2,0,1:T(8,128)(2,1)} %copy.66), calls=%async_computation.1 | async-start | bytes 1048576 | tf_op jit(solution)/shard_map/all_to_all | solution.py:120
  178.8 19.5 %all-to-all-done.1 = bf16[2,64,8,256]{3,2,0,1:T(8,128)(2,1)} async-done(((bf16[2,64,8,256]{3,2,0,1:T(8,128)(2,1)}), bf16[2,64,8,256]{3,2,0,1:T(8,128)(2,1)}, u32[]{:S(2)}, u32[]{:S(2)}) %all-to-all-start.1) | async-done | bytes 524320 | tf_op jit(solution)/shard_map/all_to_all | solution.py:120
  211.6 6.8 %all-to-all-start.4 = ((bf16[2,2,256,256]{3,1,0,2:T(2,128)(2,1)}), bf16[2,2,256,256]{3,1,0,2:T(2,128)(2,1)S(1)}, u32[]{:S(2)}, u32[]{:S(2)}) async-start(bf16[2,2,256,256]{3,1,0,2:T(2,128)(2,1)} %copy.74), calls=%async_computation.4 | async-start | bytes 1048576 | tf_op jit(solution)/shard_map/all_to_all | solution.py:133
  228.3 18.4 %all-to-all-done.4 = bf16[2,2,256,256]{3,1,0,2:T(2,128)(2,1)S(1)} async-done(((bf16[2,2,256,256]{3,1,0,2:T(2,128)(2,1)}), bf16[2,2,256,256]{3,1,0,2:T(2,128)(2,1)S(1)}, u32[]{:S(2)}, u32[]{:S(2)}) %all-to-all-start.4) | async-done | bytes 524320 | tf_op jit(solution)/shard_map/all_to_all | solution.py:133
  246.7 7.0 %all-to-all-start.9 = ((bf16[2,2,256,256]{3,1,0,2:T(2,128)(2,1)}), bf16[2,2,256,256]{3,1,0,2:T(2,128)(2,1)S(1)}, u32[]{:S(2)}, u32[]{:S(2)}) async-start(bf16[2,2,256,256]{3,1,0,2:T(2,128)(2,1)} %copy.85), calls=%async_computation.9 | async-start | bytes 1048576 | tf_op jit(solution)/shard_map/all_to_all | solution.py:139
  255.1 26.9 %all-to-all-done.9 = bf16[2,2,256,256]{3,1,0,2:T(2,128)(2,1)S(1)} async-done(((bf16[2,2,256,256]{3,1,0,2:T(2,128)(2,1)}), bf16[2,2,256,256]{3,1,0,2:T(2,128)(2,1)S(1)}, u32[]{:S(2)}, u32[]{:S(2)}) %all-to-all-start.9) | async-done | bytes 524320 | tf_op jit(solution)/shard_map/all_to_all | solution.py:139
  282.0 7.9 %all-to-all-start.7 = ((bf16[2,2,256,256]{3,1,0,2:T(2,128)(2,1)}), bf16[2,2,256,256]{3,1,0,2:T(2,128)(2,1)S(1)}, u32[]{:S(2)}, u32[]{:S(2)}) async-start(bf16[2,2,256,256]{3,1,0,2:T(2,128)(2,1)} %copy.82), calls=%async_computation.7 | async-start | bytes 1048576 | tf_op jit(solution)/shard_map/all_to_all | solution.py:136
  292.9 27.0 %all-to-all-done.7 = bf16[2,2,256,256]{3,1,0,2:T(2,128)(2,1)S(1)} async-done(((bf16[2,2,256,256]{3,1,0,2:T(2,128)(2,1)}), bf16[2,2,256,256]{3,1,0,2:T(2,128)(2,1)S(1)}, u32[]{:S(2)}, u32[]{:S(2)}) %all-to-all-start.7) | async-done | bytes 524320 | tf_op jit(solution)/shard_map/all_to_all | solution.py:136
  320.0 6.4 %all-to-all-start.5 = ((bf16[32,8,256]{2,1,0:T(8,128)(2,1)}), bf16[32,8,256]{2,1,0:T(8,128)(2,1)S(1)}, u32[]{:S(2)}, u32[]{:S(2)}) async-start(bf16[32,8,256]{2,1,0:T(8,128)(2,1)} %copy.76), calls=%async_computation.5 | async-start | bytes 262144 | tf_op jit(solution)/shard_map/all_to_all | solution.py:147
  328.9 12.2 %all-to-all-done.5 = bf16[32,8,256]{2,1,0:T(8,128)(2,1)S(1)} async-done(((bf16[32,8,256]{2,1,0:T(8,128)(2,1)}), bf16[32,8,256]{2,1,0:T(8,128)(2,1)S(1)}, u32[]{:S(2)}, u32[]{:S(2)}) %all-to-all-start.5) | async-done | bytes 131104 | tf_op jit(solution)/shard_map/all_to_all | solution.py:147
  341.1 4.7 %all-to-all-start.10 = ((bf16[32,8,256]{2,1,0:T(8,128)(2,1)}), bf16[32,8,256]{2,1,0:T(8,128)(2,1)S(1)}, u32[]{:S(2)}, u32[]{:S(2)}) async-start(bf16[32,8,256]{2,1,0:T(8,128)(2,1)} %copy.87), calls=%async_computation.10 | async-start | bytes 262144 | tf_op jit(solution)/shard_map/all_to_all | solution.py:153
  347.8 12.4 %all-to-all-done.10 = bf16[32,8,256]{2,1,0:T(8,128)(2,1)S(1)} async-done(((bf16[32,8,256]{2,1,0:T(8,128)(2,1)}), bf16[32,8,256]{2,1,0:T(8,128)(2,1)S(1)}, u32[]{:S(2)}, u32[]{:S(2)}) %all-to-all-start.10) | async-done | bytes 131104 | tf_op jit(solution)/shard_map/all_to_all | solution.py:153
  360.3 3.9 all-to-all-start.8
  365.0 13.6 %all-to-all-done.8 = bf16[32,8,256]{2,1,0:T(8,128)(2,1)S(1)} async-done(((bf16[32,8,256]{2,1,0:T(8,128)(2,1)}), bf16[32,8,256]{2,1,0:T(8,128)(2,1)S(1)}, u32[]{:S(2)}, u32[]{:S(2)}) %all-to-all-start.8) | async-done | bytes 131104 | tf_op jit(solution)/shard_map/all_to_all | solution.py:150
  379.4 76.7 %reduce-scatter.4.cloned.1.call-done = bf16[16,256]{1,0:T(8,128)(2,1)} async-done(((bf16[256,256]{1,0:T(8,128)(2,1)}), bf16[16,256]{1,0:T(8,128)(2,1)}) %reduce-scatter.4.cloned.1.call-update) | async-done | bytes 8208
  (89 shorter events, 53.9 us)
Async XLA Ops:
  36.5 15.4 %copy-start.2 = (bf16[256,256]{1,0:T(8,128)(2,1)S(1)}, bf16[256,256]{1,0:T(8,128)(2,1)}, u32[]{:S(2)}) copy-start(bf16[256,256]{1,0:T(8,128)(2,1)} %param.6) | copy-start | bytes 393220
  36.5 15.4 %copy-start.3 = (bf16[256,256]{1,0:T(8,128)(2,1)S(1)}, bf16[256,256]{1,0:T(8,128)(2,1)}, u32[]{:S(2)}) copy-start(bf16[256,256]{1,0:T(8,128)(2,1)} %param.7) | copy-start | bytes 393220
  36.5 30.6 %all-to-all-start = ((bf16[32,2,1024]{2,1,0:T(2,128)(2,1)}), bf16[32,2,1024]{2,1,0:T(2,128)(2,1)S(1)}, u32[]{:S(2)}, u32[]{:S(2)}) async-start(bf16[32,2,1024]{2,1,0:T(2,128)(2,1)} %reshape.155), calls=%async_computation | async-start | bytes 262144 | tf_op jit(solution)/shard_map/all_to_all | solution.py:106
  51.9 0.9 copy-start.4
  67.1 22.3 %all-to-all-start.2 = ((bf16[2,1,256,256]{3,0,1,2:T(2,128)(2,1)}), bf16[2,1,256,256]{3,0,1,2:T(2,128)(2,1)S(1)}, u32[]{:S(2)}, u32[]{:S(2)}) async-start(bf16[2,1,256,256]{3,0,1,2:T(2,128)(2,1)} %copy.68), calls=%async_computation.2 | async-start | bytes 524288 | tf_op jit(solution)/shard_map/all_to_all | solution.py:105
  93.6 33.6 %all-to-all-start.3 = ((bf16[2,64,8,256]{3,2,0,1:T(8,128)(2,1)}), bf16[2,64,8,256]{3,2,0,1:T(8,128)(2,1)S(1)}, u32[]{:S(2)}, u32[]{:S(2)}) async-start(bf16[2,64,8,256]{3,2,0,1:T(8,128)(2,1)} %copy.72), calls=%async_computation.3 | async-start | bytes 1048576 | tf_op jit(solution)/shard_map/all_to_all | solution.py:114
  127.2 35.8 %all-to-all-start.6 = ((bf16[2,64,8,256]{3,2,0,1:T(8,128)(2,1)}), bf16[2,64,8,256]{3,2,0,1:T(8,128)(2,1)S(1)}, u32[]{:S(2)}, u32[]{:S(2)}) async-start(bf16[2,64,8,256]{3,2,0,1:T(8,128)(2,1)} %copy.80), calls=%async_computation.6 | async-start | bytes 1048576 | tf_op jit(solution)/shard_map/all_to_all | solution.py:117
  163.0 35.3 %all-to-all-start.1 = ((bf16[2,64,8,256]{3,2,0,1:T(8,128)(2,1)}), bf16[2,64,8,256]{3,2,0,1:T(8,128)(2,1)}, u32[]{:S(2)}, u32[]{:S(2)}) async-start(bf16[2,64,8,256]{3,2,0,1:T(8,128)(2,1)} %copy.66), calls=%async_computation.1 | async-start | bytes 1048576 | tf_op jit(solution)/shard_map/all_to_all | solution.py:120
  203.6 1.2 copy-start
  203.6 1.5 copy-start.1
  211.6 35.1 %all-to-all-start.4 = ((bf16[2,2,256,256]{3,1,0,2:T(2,128)(2,1)}), bf16[2,2,256,256]{3,1,0,2:T(2,128)(2,1)S(1)}, u32[]{:S(2)}, u32[]{:S(2)}) async-start(bf16[2,2,256,256]{3,1,0,2:T(2,128)(2,1)} %copy.74), calls=%async_computation.4 | async-start | bytes 1048576 | tf_op jit(solution)/shard_map/all_to_all | solution.py:133
  246.7 35.3 %all-to-all-start.9 = ((bf16[2,2,256,256]{3,1,0,2:T(2,128)(2,1)}), bf16[2,2,256,256]{3,1,0,2:T(2,128)(2,1)S(1)}, u32[]{:S(2)}, u32[]{:S(2)}) async-start(bf16[2,2,256,256]{3,1,0,2:T(2,128)(2,1)} %copy.85), calls=%async_computation.9 | async-start | bytes 1048576 | tf_op jit(solution)/shard_map/all_to_all | solution.py:139
  282.0 38.0 %all-to-all-start.7 = ((bf16[2,2,256,256]{3,1,0,2:T(2,128)(2,1)}), bf16[2,2,256,256]{3,1,0,2:T(2,128)(2,1)S(1)}, u32[]{:S(2)}, u32[]{:S(2)}) async-start(bf16[2,2,256,256]{3,1,0,2:T(2,128)(2,1)} %copy.82), calls=%async_computation.7 | async-start | bytes 1048576 | tf_op jit(solution)/shard_map/all_to_all | solution.py:136
  320.0 21.2 %all-to-all-start.5 = ((bf16[32,8,256]{2,1,0:T(8,128)(2,1)}), bf16[32,8,256]{2,1,0:T(8,128)(2,1)S(1)}, u32[]{:S(2)}, u32[]{:S(2)}) async-start(bf16[32,8,256]{2,1,0:T(8,128)(2,1)} %copy.76), calls=%async_computation.5 | async-start | bytes 262144 | tf_op jit(solution)/shard_map/all_to_all | solution.py:147
  341.1 19.1 %all-to-all-start.10 = ((bf16[32,8,256]{2,1,0:T(8,128)(2,1)}), bf16[32,8,256]{2,1,0:T(8,128)(2,1)S(1)}, u32[]{:S(2)}, u32[]{:S(2)}) async-start(bf16[32,8,256]{2,1,0:T(8,128)(2,1)} %copy.87), calls=%async_computation.10 | async-start | bytes 262144 | tf_op jit(solution)/shard_map/all_to_all | solution.py:153
  360.3 18.3 %all-to-all-start.8 = ((bf16[32,8,256]{2,1,0:T(8,128)(2,1)}), bf16[32,8,256]{2,1,0:T(8,128)(2,1)S(1)}, u32[]{:S(2)}, u32[]{:S(2)}) async-start(bf16[32,8,256]{2,1,0:T(8,128)(2,1)} %copy.84), calls=%async_computation.8 | async-start | bytes 262144 | tf_op jit(solution)/shard_map/all_to_all | solution.py:150
  364.1 91.9 %reduce-scatter.4.cloned.1.call-start = ((), (), s32[]{:S(2)}) async-start(), calls=%async_computation.12 | async-start | bytes 139264
  365.0 13.6 %copy-start.5 = (f32[256]{0:T(256)S(1)}, f32[256]{0:T(256)}, u32[]{:S(2)}) copy-start(f32[256]{0:T(256)} %param.9) | copy-start | bytes 3076
Sparse Core Ops, SparseCore 0:
  370.1 85.8 reduce-scatter.3
where the time goes:
time: 471 us; the launch traced here: 463 us
  waiting for transfers between devices  291 us (62%)
  starting transfers between devices  77.3 us (16%)
  matrix products  30.9 us (7%)
  blocking collectives  26.5 us (6%)
  local copies, waits for them, and re-layouts  18.7 us (4%)
  between operations  14.8 us (3%)
    unnamed x2, waiting for transfers between devices  76.7 us
    all_to_all x1, waiting for transfers between devices, forward_three(): lax.all_to_all(gated_part.astype(jnp.bfloat16), 'ctx', split_axis=1, conc...  27.1 us
    all_to_all x1, waiting for transfers between devices, inverse_three(): lax.all_to_all(back_part.astype(jnp.bfloat16), 'ctx', split_axis=2, conca...  27 us
    all_to_all x1, waiting for transfers between devices, inverse_three(): lax.all_to_all(lag_part.astype(jnp.bfloat16), 'ctx', split_axis=2, concat...  26.9 us
    all_gather x1, blocking collectives, per_device(): all_filters = lax.all_gather(filters, 'mp', axis=1, tiled=True)  26.5 us
    all_to_all x1, waiting for transfers between devices, forward_three(): lax.all_to_all(value_part.astype(jnp.bfloat16), 'ctx', split_axis=1, conc...  26.4 us
    all_to_all x1, waiting for transfers between devices, forward_three(): lax.all_to_all(filter_part.astype(jnp.bfloat16), 'ctx', split_axis=1, con...  19.5 us
    all_to_all x1, waiting for transfers between devices, inverse_three(): lax.all_to_all(conv_part.astype(jnp.bfloat16), 'ctx', split_axis=2, conca...  18.4 us
  transfers between devices with their start and end apart: 12, of which 12 were waited for; matrix products, arithmetic and copies ran while one was open for 7% of the time, Pallas kernels for 0%

commit v1 on v0

v1 whole, which is shorter than its diff:
```python
import functools
import math

import jax
import jax.numpy as jnp
import numpy as np
from jax import lax
from jax.experimental import pallas as pl
from jax.experimental.pallas import tpu as pltpu
from jax.sharding import PartitionSpec as P

BLOCKS = 32
HALF = 16
MINE = 8
WIDTH = 256
LENGTH = BLOCKS * WIDTH
SHARDS = 16
FACTOR = 1.0 / math.sqrt(LENGTH)
VMEM = 32 * 1024 * 1024


def tables():
    quarter = np.arange(BLOCKS) + 0.25
    outer = 2.0 * np.pi * np.outer(quarter, np.arange(BLOCKS)) / BLOCKS
    eye = np.eye(MINE)
    cos_rows = np.kron(np.cos(outer), eye)
    sin_rows = np.kron(np.sin(outer), eye)
    first = np.concatenate([cos_rows, -sin_rows], 0)
    last = np.concatenate([cos_rows.T, sin_rows.T], 1)
    by_channel = np.arange(BLOCKS * MINE).reshape(BLOCKS, MINE).T.reshape(-1)
    inner = 2.0 * np.pi * (np.outer(np.arange(WIDTH), np.arange(WIDTH)) % WIDTH) / WIDTH
    cos_in, sin_in = (np.cos(inner), np.sin(inner))
    middle = np.block([[cos_in, -sin_in], [sin_in, cos_in]])
    twist = 2.0 * np.pi * np.outer(quarter, np.arange(WIDTH)) / LENGTH
    twist = np.repeat(twist, MINE, axis=0)
    packed = np.arange(WIDTH).reshape(2, MINE, HALF).transpose(0, 2, 1).reshape(-1)
    order = np.zeros((WIDTH, WIDTH))
    order[np.arange(WIDTH), packed] = 1.0
    twice = np.concatenate([np.eye(HALF), np.eye(HALF)], 0)
    low = lambda array: array.astype(np.float32).astype(jnp.bfloat16)
    return dict(
        first=low(first),
        first_by_channel=low(first[:, by_channel]),
        middle=low(middle),
        last=low(last),
        last_by_channel=low(last[by_channel]),
        twist_cos=np.cos(twist).astype(np.float32),
        twist_sin=np.sin(twist).astype(np.float32),
        order=low(order),
        twice=low(twice),
        eye=low(np.eye(HALF)),
    )


def dot(left, right, dims=((1,), (0,))):
    return lax.dot_general(
        left.astype(jnp.bfloat16),
        right.astype(jnp.bfloat16),
        (dims, ((), ())),
        preferred_element_type=jnp.float32,
    )


def twisted(real, imag, cos, sin):
    return jnp.concatenate([real * cos + imag * sin, imag * cos - real * sin], 1)


def forward(rows, first, middle, cos, sin):
    both = dot(first, rows)
    half = both.shape[0] // 2
    return dot(twisted(both[:half], both[half:], cos, sin), middle)


def inverse(real, imag, middle, last, cos, sin):
    both = dot(jnp.concatenate([real, imag], 1), middle)
    both = twisted(both[:, :WIDTH], both[:, WIDTH:], cos, sin)
    both = jnp.concatenate([both[:, :WIDTH], both[:, WIDTH:]], 0)
    return dot(last, both)


def parts_of(spectrum):
    return (spectrum[:, :WIDTH], spectrum[:, WIDTH:])


def pack(upper, lower, extra):
    pieces = []
    for rows in (upper, lower):
        rows = rows.reshape(BLOCKS, MINE, WIDTH)
        pieces += [rows[:, :, :128], rows[:, :, 128:]]
    shape = (BLOCKS, MINE // 2, 128)
    for piece in (extra[:, :128], extra[:, 128:]):
        pieces.append(jnp.broadcast_to(piece[:, None, :], shape))
    return jnp.concatenate(pieces, 1).astype(jnp.bfloat16)


def rows_of(block, at):
    block = block.astype(jnp.float32)
    left = block[:, at : at + MINE].reshape(BLOCKS * MINE, 128)
    right = block[:, at + MINE : at + 2 * MINE].reshape(BLOCKS * MINE, 128)
    return jnp.concatenate([left, right], 1)


def extra_of(block):
    block = block[:, 4 * MINE :].astype(jnp.float32)
    return jnp.concatenate([block[:, 0], block[:, MINE // 2]], 1)


def product_of(cotangent, gates):
    return (cotangent.astype(jnp.float32) * gates.astype(jnp.float32)).astype(jnp.bfloat16)


def outgoing(values, gates, cotangent, filters, order, twice):
    gated = product_of(cotangent, gates)
    across = ((1,), (1,))
    return pack(dot(order, values, across), dot(order, gated, across), dot(twice, filters, across))


def spectra(block, first, middle, last_by_channel, cos, sin):
    value = forward(rows_of(block, 0), first, middle, cos, sin)
    gated = forward(rows_of(block, 2 * MINE), first, middle, cos, sin)
    (value_r, value_i), (gated_r, gated_i) = (parts_of(value), parts_of(gated))
    lagged = inverse(
        gated_r * value_r + gated_i * value_i,
        gated_r * value_i - gated_i * value_r,
        middle, last_by_channel, cos, sin,
    ) * (1.0 / LENGTH)
    lagged = lagged.reshape(MINE, BLOCKS, WIDTH)
    own = jnp.broadcast_to(extra_of(block)[None], (SHARDS, BLOCKS, WIDTH))
    sent = jnp.concatenate([jnp.concatenate([lagged, lagged], 0), own], 1).astype(jnp.bfloat16)
    return (value, gated, sent)


def results(filters, lagged, value, gated, first_by_channel, middle, last, cos, sin):
    filt = forward(filters.reshape(MINE * BLOCKS, WIDTH), first_by_channel, middle, cos, sin)
    (filt_r, filt_i) = parts_of(filt)
    (value_r, value_i), (gated_r, gated_i) = (parts_of(value), parts_of(gated))
    scale = FACTOR / LENGTH
    conv = inverse(
        filt_r * value_r - filt_i * value_i,
        -filt_r * value_i - filt_i * value_r,
        middle, last, cos, sin,
    ) * scale
    back = inverse(
        filt_r * gated_r + filt_i * gated_i,
        filt_i * gated_r - filt_r * gated_i,
        middle, last, cos, sin,
    ) * scale
    total = lagged.astype(jnp.float32).sum(0) * FACTOR
    return pack(conv, back, total)


def finished(block, mine, values, gates, cotangent, skip_row, order, eye):
    down = ((0,), (0,))
    conv = dot(rows_of(block, 0), order, down)
    back = dot(rows_of(block, 2 * MINE), order, down)
    gated = product_of(cotangent, gates).astype(jnp.float32)
    grad_gates = cotangent.astype(jnp.float32) * (conv + skip_row * values.astype(jnp.float32))
    grad_values = back + skip_row * gated
    grad_filters = dot(extra_of(mine), eye, down)
    return tuple(out.astype(jnp.bfloat16) for out in (grad_gates, grad_values, grad_filters))


def outgoing_kernel(*refs):
    refs[-1][...] = outgoing(*(ref[...] for ref in refs[:-1]))


def spectra_kernel(*refs):
    outs = spectra(*(ref[...] for ref in refs[:-3]))
    for ref, out in zip(refs[-3:], outs):
        ref[...] = out


def results_kernel(place, arrived, *refs):
    start = pl.multiple_of(place[0] * MINE, MINE)
    filters = arrived[pl.ds(start, MINE), BLOCKS:, :]
    lagged = arrived[:, :BLOCKS, :]
    refs[-1][...] = results(filters, lagged, *(ref[...] for ref in refs[:-1]))


def finished_kernel(place, block, *refs):
    start = pl.multiple_of(place[0] * HALF, HALF)
    mine = block[pl.ds(start, HALF)]
    outs = finished(block[...], mine, *(ref[...] for ref in refs[:-3]))
    for ref, out in zip(refs[-3:], outs):
        ref[...] = out


def call(kernel, outs, args, flops, scalars=0):
    whole = pl.BlockSpec(memory_space=pltpu.VMEM)
    scalar = pl.BlockSpec(memory_space=pltpu.SMEM)
    size = sum(math.prod(out.shape) * out.dtype.itemsize for out in (*outs, *args))
    single = len(outs) == 1
    return pl.pallas_call(
        kernel,
        out_shape=outs[0] if single else outs,
        in_specs=[scalar] * scalars + [whole] * (len(args) - scalars),
        out_specs=whole if single else (whole,) * len(outs),
        compiler_params=pltpu.CompilerParams(vmem_limit_bytes=VMEM),
        cost_estimate=pl.CostEstimate(flops=flops, bytes_accessed=size, transcendentals=0),
    )(*args)


def swap(block, axis):
    return lax.all_to_all(block, axis, split_axis=0, concat_axis=0, tiled=True)


def per_device(table, values, gates, cotangent, filters, skip_gain):
    shape = functools.partial(jax.ShapeDtypeStruct, dtype=jnp.bfloat16)
    spectrum = jax.ShapeDtypeStruct((WIDTH, 2 * WIDTH), jnp.float32)
    packed = shape((BLOCKS, 5 * MINE, 128))
    ctx_half = (lax.axis_index("ctx") // HALF).astype(jnp.int32).reshape(1)
    mp_half = (lax.axis_index("mp") // MINE).astype(jnp.int32).reshape(1)
    twist = (table["twist_cos"], table["twist_sin"])
    cube = 2 * WIDTH**3

    block = call(
        outgoing_kernel, (packed,),
        (values, gates, cotangent, filters, table["order"], table["twice"]), 2 * cube,
    )
    block = swap(block, "ctx")
    value, gated, sent = call(
        spectra_kernel, (spectrum, spectrum, shape((SHARDS, 2 * BLOCKS, WIDTH))),
        (block, table["first"], table["middle"], table["last_by_channel"], *twist), 18 * cube,
    )
    sent = swap(sent, "mp")
    block = call(
        results_kernel, (packed,),
        (ctx_half, sent, value, gated, table["first_by_channel"], table["middle"], table["last"], *twist),
        18 * cube, scalars=1,
    )
    block = swap(block, "ctx")
    return call(
        finished_kernel, (shape(values.shape), shape(values.shape), shape(filters.shape)),
        (mp_half, block, values, gates, cotangent, skip_gain[None, :], table["order"], table["eye"]),
        2 * cube, scalars=1,
    )


def solution(mesh):
    return jax.shard_map(
        functools.partial(per_device, tables()),
        mesh=mesh,
        in_specs=(P("ctx", "mp"), P("ctx", "mp"), P("ctx", "mp"), P("ctx", "mp"), P("mp")),
        out_specs=(P("ctx", "mp"), P("ctx", "mp"), P("ctx", "mp")),
        check_vma=False,
    )
```

time: 471 us -> 100 us (0.21); the launches traced: 463 us -> 98.7 us
  waiting for transfers between devices: 291 us -> 33.3 us
  starting transfers between devices: 77.3 us -> 14 us
  matrix products: 30.9 us -> 0 us
  between operations: 14.8 us -> 0.75 us
  blocking collectives: 26.5 us -> 39.4 us
  local copies, waits for them, and re-layouts: 18.7 us -> 5.82 us
  Pallas kernels: 0 us -> 5.45 us
    all_to_all x11 -> x2, waiting for transfers between devices: 214 us -> 33.3 us  [swap(): return lax.all_to_all(block, axis, split_axis=0, concat_axis=0, tiled=True)]
    unnamed x2 -> x0, waiting for transfers between devices: 76.7 us -> none
    all_to_all x11 -> x2, starting transfers between devices: 77.2 us -> 14 us  [swap(): return lax.all_to_all(block, axis, split_axis=0, concat_axis=0, tiled=True)]
    all_to_all x0 -> x1, blocking collectives: none -> 39.4 us  [swap(): return lax.all_to_all(block, axis, split_axis=0, concat_axis=0, tiled=True)]
    dot_general x24 -> x0, matrix products: 30.9 us -> none  [the longest x3 6.67 us: finish_forward(): jnp.einsum('skbc,bm->skmc', partial_value, sin_inner, precision=lax.Preci...]
    all_gather x1 -> x0, blocking collectives: 26.5 us -> none  [per_device(): all_filters = lax.all_gather(filters, 'mp', axis=1, tiled=True)]
    another operation x6 -> x0, local copies, waits for them, and re-layouts: 7.32 us -> none  [the longest x3 4.04 us: start_inverse(): jnp.stack([real_part * cos_twist - imag_part * sin_twist, imag_part * cos...]
    pallas_call x0 -> x4, Pallas kernels: none -> 5.45 us  [call(): pl.pallas_call(kernel, out_shape=outs[0] if single else outs, in_specs=[s...]
  transfers between devices with their start and end apart: 12 -> 2, of which waited for: 12 -> 2; matrix products, arithmetic and copies ran while one was open for 7% -> 0% of each run, Pallas kernels for 0% -> 0%
where the time goes in v1:
time: 100 us; the launch traced here: 98.7 us
  blocking collectives  39.4 us (39%)
  waiting for transfers between devices  33.3 us (33%)
  starting transfers between devices  14 us (14%)
  local copies, waits for them, and re-layouts  5.82 us (6%)
  Pallas kernels  5.45 us (5%)
    all_to_all x1, blocking collectives, swap(): return lax.all_to_all(block, axis, split_axis=0, concat_axis=0, tiled=True)  39.4 us
    all_to_all x2, waiting for transfers between devices, swap(): return lax.all_to_all(block, axis, split_axis=0, concat_axis=0, tiled=True)  33.3 us
    all_to_all x2, starting transfers between devices, swap(): return lax.all_to_all(block, axis, split_axis=0, concat_axis=0, tiled=True)  14 us
    pallas_call x4, Pallas kernels, call(): pl.pallas_call(kernel, out_shape=outs[0] if single else outs, in_specs=[s...  5.45 us
    unnamed x37, local copies, waits for them, and re-layouts  5.14 us
  transfers between devices with their start and end apart: 2, of which 2 were waited for; matrix products, arithmetic and copies ran while one was open for 0% of the time, Pallas kernels for 0%

profile of v1, /device:TPU:1, one launch (start us, length us, event | category | flops | bytes accessed | tf_op | source)
XLA Modules:
  0.0 98.7 jit_solution(4581055639446466223)
XLA Ops:
  0.6 0.0 copy-start.13
  0.6 0.8 copy.18.refs_3_
  1.5 0.0 copy-start
  1.5 0.9 copy-done
  2.4 0.9 copy-done.2
  3.3 0.9 copy-done.4
  4.2 0.9 copy-done.6
  5.1 0.3 shard_map.166
  5.4 0.0 copy-start.8
  5.4 39.4 %all_to_all.15.refs_0_ = bf16[32,40,128]{2,1,0:T(8,128)(2,1)S(1)} all-to-all(bf16[32,40,128]{2,1,0:T(8,128)(2,1)S(1)} %shard_map.166), channel_id=1, replica_groups=mesh['ctx'=32,'mp'=16] {'ctx'}, dimensions={0} | all-to-all | bytes 655360 | tf_op jit(solution)/shard_map/all_to_all | solution.py:204
  44.8 0.0 copy-done.16
  44.8 0.0 copy-done.17
  44.8 0.0 copy-done.8
  44.8 2.1 %shard_map.167 = (f32[256,512]{1,0:T(8,128)S(1)}, f32[256,512]{1,0:T(8,128)S(1)}, bf16[16,64,256]{2,1,0:T(8,128)(2,1)}) custom-call(bf16[32,40,128]{2,1,0:T(8,128)(2,1)S(1)} %all_to_all.15.refs_0_, bf16[512,256]{1,0:T(8,128)(2,1)S(1)} %copy-done.17, bf16[512,512]{1,0:T(8,128)(2,1)S(1)} %copy-done.8, bf16[256,512]{1,0:T(8,128)(2,1)S(1)} %copy-done.16, ...), custom_call_target="tpu_custom_call" | custom-call | flops 603979776 | bytes 3473408 | tf_op jit(solution)/shard_map/pallas_call | solution.py:193
  46.9 9.9 %all-to-all-start.1 = ((bf16[16,64,256]{2,1,0:T(8,128)(2,1)}), bf16[16,64,256]{2,1,0:T(8,128)(2,1)S(1)}, u32[]{:S(2)}, u32[]{:S(2)}) async-start(bf16[16,64,256]{2,1,0:T(8,128)(2,1)} %get-tuple-element.6), calls=%async_computation.1 | async-start | bytes 1048576 | tf_op jit(solution)/shard_map/all_to_all | solution.py:204
  56.9 11.3 %all-to-all-done.1.arrived = bf16[16,64,256]{2,1,0:T(8,128)(2,1)S(1)} async-done(((bf16[16,64,256]{2,1,0:T(8,128)(2,1)}), bf16[16,64,256]{2,1,0:T(8,128)(2,1)S(1)}, u32[]{:S(2)}, u32[]{:S(2)}) %all-to-all-start.1) | async-done | bytes 524320 | tf_op jit(solution)/shard_map/all_to_all | solution.py:204
  68.2 0.0 copy-done.11
  68.2 2.1 %shard_map.168 = bf16[32,40,128]{2,1,0:T(8,128)(2,1)} custom-call(s32[1]{0:T(128)} %bitcast.1.place, bf16[16,64,256]{2,1,0:T(8,128)(2,1)S(1)} %all-to-all-done.1.arrived, f32[256,512]{1,0:T(8,128)S(1)} %get-tuple-element.7.refs_0_, f32[256,512]{1,0:T(8,128)S(1)} %get-tuple-element.8.refs_1_, bf16[512,256]{1,0:T(8,128)(2,1)S(1)} %copy-done.12, ...), custom_call_target="tpu_custom_call" | custom-call | flops 603979776 | bytes 3473412 | tf_op jit(solution)/shard_map/pallas_call | solution.py:193
  70.3 4.0 %all-to-all-start.2 = ((bf16[32,40,128]{2,1,0:T(8,128)(2,1)}), bf16[32,40,128]{2,1,0:T(8,128)(2,1)S(1)}, u32[]{:S(2)}, u32[]{:S(2)}) async-start(bf16[32,40,128]{2,1,0:T(8,128)(2,1)} %shard_map.168), calls=%async_computation.2 | async-start | bytes 655360 | tf_op jit(solution)/shard_map/all_to_all | solution.py:204
  74.3 0.0 copy-start.14
  74.3 22.0 %all-to-all-done.2.block = bf16[32,40,128]{2,1,0:T(8,128)(2,1)S(1)} async-done(((bf16[32,40,128]{2,1,0:T(8,128)(2,1)}), bf16[32,40,128]{2,1,0:T(8,128)(2,1)S(1)}, u32[]{:S(2)}, u32[]{:S(2)}) %all-to-all-start.2) | async-done | bytes 327712 | tf_op jit(solution)/shard_map/all_to_all | solution.py:204
  96.4 0.6 copy-done.15
  97.1 1.0 shard_map.169
  98.0 0.7 copy.19
  (23 shorter events, 0.0 us)
Async XLA Ops:
  0.6 0.8 copy-start.13
  1.5 0.9 copy-start
  2.4 0.9 copy-start.2
  3.3 0.9 copy-start.4
  4.2 0.9 copy-start.6
  5.1 39.7 %copy-start.9 = (f32[256,256]{1,0:T(8,128)S(1)}, f32[256,256]{1,0:T(8,128)}, u32[]{:S(2)}) copy-start(f32[256,256]{1,0:T(8,128)} %constant.62.clone.refs_5_.refs_6_) | copy-start | bytes 786436
  5.1 39.7 %copy-start.10 = (f32[256,256]{1,0:T(8,128)S(1)}, f32[256,256]{1,0:T(8,128)}, u32[]{:S(2)}) copy-start(f32[256,256]{1,0:T(8,128)} %constant.61.clone.refs_4_.refs_5_) | copy-start | bytes 786436
  5.1 39.7 %copy-start.16 = (bf16[256,512]{1,0:T(8,128)(2,1)S(1)}, bf16[256,512]{1,0:T(8,128)(2,1)}, u32[]{:S(2)}) copy-start(bf16[256,512]{1,0:T(8,128)(2,1)} %constant.60.clone.refs_3_) | copy-start | bytes 786436
  5.1 39.7 %copy-start.17 = (bf16[512,256]{1,0:T(8,128)(2,1)S(1)}, bf16[512,256]{1,0:T(8,128)(2,1)}, u32[]{:S(2)}) copy-start(bf16[512,256]{1,0:T(8,128)(2,1)} %constant.58.clone.refs_1_) | copy-start | bytes 786436
  5.4 39.4 %copy-start.8 = (bf16[512,512]{1,0:T(8,128)(2,1)S(1)}, bf16[512,512]{1,0:T(8,128)(2,1)}, u32[]{:S(2)}) copy-start(bf16[512,512]{1,0:T(8,128)(2,1)} %constant.59.clone.refs_2_.refs_3_) | copy-start | bytes 1572868
  46.9 21.2 %copy-start.11 = (bf16[256,512]{1,0:T(8,128)(2,1)S(1)}, bf16[256,512]{1,0:T(8,128)(2,1)}, u32[]{:S(2)}) copy-start(bf16[256,512]{1,0:T(8,128)(2,1)} %constant.64.clone.refs_4_) | copy-start | bytes 786436
  46.9 21.2 %copy-start.12 = (bf16[512,256]{1,0:T(8,128)(2,1)S(1)}, bf16[512,256]{1,0:T(8,128)(2,1)}, u32[]{:S(2)}) copy-start(bf16[512,256]{1,0:T(8,128)(2,1)} %constant.63.clone.refs_2_) | copy-start | bytes 786436
  46.9 21.2 %all-to-all-start.1 = ((bf16[16,64,256]{2,1,0:T(8,128)(2,1)}), bf16[16,64,256]{2,1,0:T(8,128)(2,1)S(1)}, u32[]{:S(2)}, u32[]{:S(2)}) async-start(bf16[16,64,256]{2,1,0:T(8,128)(2,1)} %get-tuple-element.6), calls=%async_computation.1 | async-start | bytes 1048576 | tf_op jit(solution)/shard_map/all_to_all | solution.py:204
  70.3 26.1 %copy-start.1 = (bf16[256,256]{1,0:T(8,128)(2,1)S(1)}, bf16[256,256]{1,0:T(8,128)(2,1)}, u32[]{:S(2)}) copy-start(bf16[256,256]{1,0:T(8,128)(2,1)} %refs_0_.3) | copy-start | bytes 393220
  70.3 26.1 %copy-start.3 = (bf16[256,256]{1,0:T(8,128)(2,1)S(1)}, bf16[256,256]{1,0:T(8,128)(2,1)}, u32[]{:S(2)}) copy-start(bf16[256,256]{1,0:T(8,128)(2,1)} %refs_1_.4) | copy-start | bytes 393220
  70.3 26.1 %copy-start.5 = (bf16[256,256]{1,0:T(8,128)(2,1)S(1)}, bf16[256,256]{1,0:T(8,128)(2,1)}, u32[]{:S(2)}) copy-start(bf16[256,256]{1,0:T(8,128)(2,1)} %refs_2_.5) | copy-start | bytes 393220
  70.3 26.1 %copy-start.7 = (bf16[256,256]{1,0:T(8,128)(2,1)S(1)}, bf16[256,256]{1,0:T(8,128)(2,1)}, u32[]{:S(2)}) copy-start(bf16[256,256]{1,0:T(8,128)(2,1)} %constant.56.clone.refs_4_) | copy-start | bytes 393220
  70.3 26.1 %all-to-all-start.2 = ((bf16[32,40,128]{2,1,0:T(8,128)(2,1)}), bf16[32,40,128]{2,1,0:T(8,128)(2,1)S(1)}, u32[]{:S(2)}, u32[]{:S(2)}) async-start(bf16[32,40,128]{2,1,0:T(8,128)(2,1)} %shard_map.168), calls=%async_computation.2 | async-start | bytes 655360 | tf_op jit(solution)/shard_map/all_to_all | solution.py:204
  74.3 22.1 %copy-start.14 = (bf16[16,16]{1,0:T(8,128)(2,1)S(1)}, bf16[16,16]{1,0:T(8,128)(2,1)}, u32[]{:S(2)}) copy-start(bf16[16,16]{1,0:T(8,128)(2,1)} %constant.65.clone.refs_5_) | copy-start | bytes 1540
  96.4 0.7 copy-start.15

commit v2 on v1

--- a/solution.py
+++ b/solution.py
@@ -33,10 +33,6 @@
     middle = np.block([[cos_in, -sin_in], [sin_in, cos_in]])
     twist = 2.0 * np.pi * np.outer(quarter, np.arange(WIDTH)) / LENGTH
     twist = np.repeat(twist, MINE, axis=0)
-    packed = np.arange(WIDTH).reshape(2, MINE, HALF).transpose(0, 2, 1).reshape(-1)
-    order = np.zeros((WIDTH, WIDTH))
-    order[np.arange(WIDTH), packed] = 1.0
-    twice = np.concatenate([np.eye(HALF), np.eye(HALF)], 0)
     low = lambda array: array.astype(np.float32).astype(jnp.bfloat16)
     return dict(
         first=low(first),
@@ -46,9 +42,6 @@
         last_by_channel=low(last[by_channel]),
         twist_cos=np.cos(twist).astype(np.float32),
         twist_sin=np.sin(twist).astype(np.float32),
-        order=low(order),
-        twice=low(twice),
-        eye=low(np.eye(HALF)),
     )
 
 
@@ -59,6 +52,13 @@
         (dims, ((), ())),
         preferred_element_type=jnp.float32,
     )
+
+
+def order_of():
+    row = lax.broadcasted_iota(jnp.int32, (WIDTH, WIDTH), 0)
+    channel = lax.broadcasted_iota(jnp.int32, (WIDTH, WIDTH), 1)
+    wanted = ((row >> 7) << 7) + ((row & 7) << 4) + ((row >> 3) & 15)
+    return (channel == wanted).astype(jnp.float32).astype(jnp.bfloat16)
 
 
 def twisted(real, imag, cos, sin):
@@ -109,10 +109,12 @@
     return (cotangent.astype(jnp.float32) * gates.astype(jnp.float32)).astype(jnp.bfloat16)
 
 
-def outgoing(values, gates, cotangent, filters, order, twice):
+def outgoing(values, gates, cotangent, filters):
     gated = product_of(cotangent, gates)
     across = ((1,), (1,))
-    return pack(dot(order, values, across), dot(order, gated, across), dot(twice, filters, across))
+    order = order_of()
+    twice = jnp.concatenate([filters, filters], 0).astype(jnp.float32)
+    return pack(dot(order, values, across), dot(order, gated, across), twice)
 
 
 def spectra(block, first, middle, last_by_channel, cos, sin):
@@ -149,19 +151,28 @@
     return pack(conv, back, total)
 
 
-def finished(block, mine, values, gates, cotangent, skip_row, order, eye):
+def finished(block, mine, values, gates, cotangent, skip_row):
     down = ((0,), (0,))
+    order = order_of()
     conv = dot(rows_of(block, 0), order, down)
     back = dot(rows_of(block, 2 * MINE), order, down)
     gated = product_of(cotangent, gates).astype(jnp.float32)
     grad_gates = cotangent.astype(jnp.float32) * (conv + skip_row * values.astype(jnp.float32))
     grad_values = back + skip_row * gated
-    grad_filters = dot(extra_of(mine), eye, down)
+    grad_filters = extra_of(mine)
     return tuple(out.astype(jnp.bfloat16) for out in (grad_gates, grad_values, grad_filters))
 
 
-def outgoing_kernel(*refs):
-    refs[-1][...] = outgoing(*(ref[...] for ref in refs[:-1]))
+def outgoing_kernel(values, gates, cotangent, filters, skip, out, skip_out, *scratch):
+    held, sems = (scratch[:-1], scratch[-1])
+    copies = []
+    for at, (source, target) in enumerate(zip((values, gates, cotangent, filters, skip), held)):
+        copies.append(pltpu.make_async_copy(source, target, sems.at[at]))
+        copies[-1].start()
+    for copy in copies:
+        copy.wait()
+    out[...] = outgoing(*(ref[...] for ref in held[:-1]))
+    skip_out[...] = held[-1][...]
 
 
 def spectra_kernel(*refs):
@@ -185,16 +196,22 @@
         ref[...] = out
 
 
-def call(kernel, outs, args, flops, scalars=0):
+def call(kernel, outs, args, flops, scalars=0, fetched=False):
     whole = pl.BlockSpec(memory_space=pltpu.VMEM)
     scalar = pl.BlockSpec(memory_space=pltpu.SMEM)
+    given = pl.BlockSpec(memory_space=pl.ANY) if fetched else whole
     size = sum(math.prod(out.shape) * out.dtype.itemsize for out in (*outs, *args))
     single = len(outs) == 1
+    scratch = []
+    if fetched:
+        scratch = [pltpu.VMEM(arg.shape, arg.dtype) for arg in args]
+        scratch.append(pltpu.SemaphoreType.DMA((len(args),)))
     return pl.pallas_call(
         kernel,
         out_shape=outs[0] if single else outs,
-        in_specs=[scalar] * scalars + [whole] * (len(args) - scalars),
+        in_specs=[scalar] * scalars + [given] * (len(args) - scalars),
         out_specs=whole if single else (whole,) * len(outs),
+        scratch_shapes=scratch,
         compiler_params=pltpu.CompilerParams(vmem_limit_bytes=VMEM),
         cost_estimate=pl.CostEstimate(flops=flops, bytes_accessed=size, transcendentals=0),
     )(*args)
@@ -213,9 +230,10 @@
     twist = (table["twist_cos"], table["twist_sin"])
     cube = 2 * WIDTH**3
 
-    block = call(
-        outgoing_kernel, (packed,),
-        (values, gates, cotangent, filters, table["order"], table["twice"]), 2 * cube,
+    skip_shape = jax.ShapeDtypeStruct((1, WIDTH), jnp.float32)
+    block, skip_row = call(
+        outgoing_kernel, (packed, skip_shape),
+        (values, gates, cotangent, filters.T, skip_gain[None, :]), 2 * cube, fetched=True,
     )
     block = swap(block, "ctx")
     value, gated, sent = call(
@@ -229,11 +247,11 @@
         18 * cube, scalars=1,
     )
     block = swap(block, "ctx")
-    return call(
-        finished_kernel, (shape(values.shape), shape(values.shape), shape(filters.shape)),
-        (mp_half, block, values, gates, cotangent, skip_gain[None, :], table["order"], table["eye"]),
-        2 * cube, scalars=1,
-    )
+    grad_gates, grad_values, grad_filters = call(
+        finished_kernel, (shape(values.shape), shape(values.shape), shape((HALF, WIDTH))),
+        (mp_half, block, values, gates, cotangent, skip_row), 2 * cube, scalars=1,
+    )
+    return (grad_gates, grad_values, grad_filters.T)
 
 
 def solution(mesh):

time: 100 us -> 101 us (1.010)
    unnamed x37 -> x30, local copies, waits for them, and re-layouts: 5.14 us -> 6.01 us
where the time goes in v2:
time: 101 us; the launch traced here: 99.4 us
  blocking collectives  39.4 us (39%)
  waiting for transfers between devices  33.3 us (33%)
  starting transfers between devices  13.9 us (14%)
  local copies, waits for them, and re-layouts  6.01 us (6%)
  Pallas kernels  5.98 us (6%)
    all_to_all x1, blocking collectives, swap(): return lax.all_to_all(block, axis, split_axis=0, concat_axis=0, tiled=True)  39.4 us
    all_to_all x2, waiting for transfers between devices, swap(): return lax.all_to_all(block, axis, split_axis=0, concat_axis=0, tiled=True)  33.3 us
    all_to_all x2, starting transfers between devices, swap(): return lax.all_to_all(block, axis, split_axis=0, concat_axis=0, tiled=True)  13.9 us
    unnamed x30, local copies, waits for them, and re-layouts  6.01 us
    pallas_call x4, Pallas kernels, call(): pl.pallas_call(kernel, out_shape=outs[0] if single else outs, in_specs=[s...  5.98 us
  transfers between devices with their start and end apart: 2, of which 2 were waited for; matrix products, arithmetic and copies ran while one was open for 0% of the time, Pallas kernels for 0%

profile of v2, /device:TPU:1, one launch (start us, length us, event | category | flops | bytes accessed | tf_op | source)
XLA Modules:
  0.0 99.4 jit_solution(17819125543490611646)
XLA Ops:
  0.6 0.0 copy-start.12
  0.6 0.7 copy-done.12
  1.3 0.9 copy-done
  2.2 0.9 copy-done.2
  3.1 0.9 copy-done.4
  4.0 0.7 copy-done.11
  4.7 0.8 shard_map.139
  5.5 0.0 copy-start.7
  5.6 0.0 copy-start.8
  5.6 39.4 %all_to_all.15.refs_0_ = bf16[32,40,128]{2,1,0:T(8,128)(2,1)S(1)} all-to-all(bf16[32,40,128]{2,1,0:T(8,128)(2,1)S(1)} %get-tuple-element.11), channel_id=1, replica_groups=mesh['ctx'=32,'mp'=16] {'ctx'}, dimensions={0} | all-to-all | bytes 655360 | tf_op jit(solution)/shard_map/all_to_all | solution.py:221
  45.0 0.0 copy-done.6
  45.0 0.0 copy-done.7
  45.0 0.0 copy-start.13
  45.0 0.9 copy-done.13
  45.9 0.9 copy-done.14
  46.9 2.1 %shard_map.140 = (f32[256,512]{1,0:T(8,128)S(1)}, f32[256,512]{1,0:T(8,128)S(1)}, bf16[16,64,256]{2,1,0:T(8,128)(2,1)}) custom-call(bf16[32,40,128]{2,1,0:T(8,128)(2,1)S(1)} %all_to_all.15.refs_0_, bf16[512,256]{1,0:T(8,128)(2,1)S(1)} %copy-done.14, bf16[512,512]{1,0:T(8,128)(2,1)S(1)} %copy-done.6, bf16[256,512]{1,0:T(8,128)(2,1)S(1)} %copy-done.13, ...), custom_call_target="tpu_custom_call" | custom-call | flops 603979776 | bytes 3473408 | tf_op jit(solution)/shard_map/pallas_call | solution.py:209
  49.0 9.9 %all-to-all-start.1 = ((bf16[16,64,256]{2,1,0:T(8,128)(2,1)}), bf16[16,64,256]{2,1,0:T(8,128)(2,1)S(1)}, u32[]{:S(2)}, u32[]{:S(2)}) async-start(bf16[16,64,256]{2,1,0:T(8,128)(2,1)} %get-tuple-element.12), calls=%async_computation.1 | async-start | bytes 1048576 | tf_op jit(solution)/shard_map/all_to_all | solution.py:221
  58.9 11.3 %all-to-all-done.1.arrived = bf16[16,64,256]{2,1,0:T(8,128)(2,1)S(1)} async-done(((bf16[16,64,256]{2,1,0:T(8,128)(2,1)}), bf16[16,64,256]{2,1,0:T(8,128)(2,1)S(1)}, u32[]{:S(2)}, u32[]{:S(2)}) %all-to-all-start.1) | async-done | bytes 524320 | tf_op jit(solution)/shard_map/all_to_all | solution.py:221
  70.2 0.0 copy-done.10
  70.2 2.1 %shard_map.141 = bf16[32,40,128]{2,1,0:T(8,128)(2,1)} custom-call(s32[1]{0:T(128)} %bitcast.1.place, bf16[16,64,256]{2,1,0:T(8,128)(2,1)S(1)} %all-to-all-done.1.arrived, f32[256,512]{1,0:T(8,128)S(1)} %get-tuple-element.13.refs_0_, f32[256,512]{1,0:T(8,128)S(1)} %get-tuple-element.14.refs_1_, bf16[512,256]{1,0:T(8,128)(2,1)S(1)} %copy-done.10, ...), custom_call_target="tpu_custom_call" | custom-call | flops 603979776 | bytes 3473412 | tf_op jit(solution)/shard_map/pallas_call | solution.py:209
  72.3 4.0 %all-to-all-start.2 = ((bf16[32,40,128]{2,1,0:T(8,128)(2,1)}), bf16[32,40,128]{2,1,0:T(8,128)(2,1)S(1)}, u32[]{:S(2)}, u32[]{:S(2)}) async-start(bf16[32,40,128]{2,1,0:T(8,128)(2,1)} %shard_map.141), calls=%async_computation.2 | async-start | bytes 655360 | tf_op jit(solution)/shard_map/all_to_all | solution.py:221
  76.3 22.0 %all-to-all-done.2.block = bf16[32,40,128]{2,1,0:T(8,128)(2,1)S(1)} async-done(((bf16[32,40,128]{2,1,0:T(8,128)(2,1)}), bf16[32,40,128]{2,1,0:T(8,128)(2,1)S(1)}, u32[]{:S(2)}, u32[]{:S(2)}) %all-to-all-start.2) | async-done | bytes 327712 | tf_op jit(solution)/shard_map/all_to_all | solution.py:221
  98.4 0.0 copy-done.1
  98.4 1.0 shard_map.142
  (15 shorter events, 0.0 us)
Async XLA Ops:
  0.6 0.7 copy-start.12
  1.3 0.9 copy-start
  2.2 0.9 copy-start.2
  3.1 0.9 copy-start.4
  4.0 0.7 copy-start.11
  4.7 40.2 %copy-start.6 = (bf16[512,512]{1,0:T(8,128)(2,1)S(1)}, bf16[512,512]{1,0:T(8,128)(2,1)}, u32[]{:S(2)}) copy-start(bf16[512,512]{1,0:T(8,128)(2,1)} %constant.51.clone.refs_2_.refs_3_) | copy-start | bytes 1572868
  5.5 39.4 %copy-start.7 = (f32[256,256]{1,0:T(8,128)S(1)}, f32[256,256]{1,0:T(8,128)}, u32[]{:S(2)}) copy-start(f32[256,256]{1,0:T(8,128)} %constant.54.clone.refs_5_.refs_6_) | copy-start | bytes 786436
  5.6 39.4 %copy-start.8 = (f32[256,256]{1,0:T(8,128)S(1)}, f32[256,256]{1,0:T(8,128)}, u32[]{:S(2)}) copy-start(f32[256,256]{1,0:T(8,128)} %constant.53.clone.refs_4_.refs_5_) | copy-start | bytes 786436
  45.0 1.0 copy-start.13
  45.9 0.9 copy-start.14
  49.0 21.2 %copy-start.9 = (bf16[256,512]{1,0:T(8,128)(2,1)S(1)}, bf16[256,512]{1,0:T(8,128)(2,1)}, u32[]{:S(2)}) copy-start(bf16[256,512]{1,0:T(8,128)(2,1)} %constant.56.clone.refs_4_) | copy-start | bytes 786436
  49.0 21.2 %copy-start.10 = (bf16[512,256]{1,0:T(8,128)(2,1)S(1)}, bf16[512,256]{1,0:T(8,128)(2,1)}, u32[]{:S(2)}) copy-start(bf16[512,256]{1,0:T(8,128)(2,1)} %constant.55.clone.refs_2_) | copy-start | bytes 786436
  49.0 21.2 %all-to-all-start.1 = ((bf16[16,64,256]{2,1,0:T(8,128)(2,1)}), bf16[16,64,256]{2,1,0:T(8,128)(2,1)S(1)}, u32[]{:S(2)}, u32[]{:S(2)}) async-start(bf16[16,64,256]{2,1,0:T(8,128)(2,1)} %get-tuple-element.12), calls=%async_computation.1 | async-start | bytes 1048576 | tf_op jit(solution)/shard_map/all_to_all | solution.py:221
  72.3 26.1 %copy-start.1 = (bf16[256,256]{1,0:T(8,128)(2,1)S(1)}, bf16[256,256]{1,0:T(8,128)(2,1)}, u32[]{:S(2)}) copy-start(bf16[256,256]{1,0:T(8,128)(2,1)} %refs_0_.1) | copy-start | bytes 393220
  72.3 26.1 %copy-start.3 = (bf16[256,256]{1,0:T(8,128)(2,1)S(1)}, bf16[256,256]{1,0:T(8,128)(2,1)}, u32[]{:S(2)}) copy-start(bf16[256,256]{1,0:T(8,128)(2,1)} %refs_1_.2) | copy-start | bytes 393220
  72.3 26.1 %copy-start.5 = (bf16[256,256]{1,0:T(8,128)(2,1)S(1)}, bf16[256,256]{1,0:T(8,128)(2,1)}, u32[]{:S(2)}) copy-start(bf16[256,256]{1,0:T(8,128)(2,1)} %refs_2_.3) | copy-start | bytes 393220
  72.3 26.1 %all-to-all-start.2 = ((bf16[32,40,128]{2,1,0:T(8,128)(2,1)}), bf16[32,40,128]{2,1,0:T(8,128)(2,1)S(1)}, u32[]{:S(2)}, u32[]{:S(2)}) async-start(bf16[32,40,128]{2,1,0:T(8,128)(2,1)} %shard_map.141), calls=%async_computation.2 | async-start | bytes 655360 | tf_op jit(solution)/shard_map/all_to_all | solution.py:221

commit v3 on v2

v3 whole, which is shorter than its diff:
```python
import functools
import math

import jax
import jax.numpy as jnp
import numpy as np
from jax import lax
from jax.experimental import pallas as pl
from jax.experimental.pallas import tpu as pltpu
from jax.sharding import PartitionSpec as P

BLOCKS = 32
HALF = 16
MINE = 8
WIDTH = 256
LENGTH = BLOCKS * WIDTH
SHARDS = 16
FACTOR = 1.0 / math.sqrt(LENGTH)
VMEM = 32 * 1024 * 1024
MOST = 63 * 1024 * 1024


def tables():
    quarter = np.arange(BLOCKS) + 0.25
    outer = 2.0 * np.pi * np.outer(quarter, np.arange(BLOCKS)) / BLOCKS
    eye = np.eye(MINE)
    cos_rows = np.kron(np.cos(outer), eye)
    sin_rows = np.kron(np.sin(outer), eye)
    first = np.concatenate([cos_rows, -sin_rows], 0)
    last = np.concatenate([cos_rows.T, sin_rows.T], 1)
    by_channel = np.arange(BLOCKS * MINE).reshape(BLOCKS, MINE).T.reshape(-1)
    inner = 2.0 * np.pi * (np.outer(np.arange(WIDTH), np.arange(WIDTH)) % WIDTH) / WIDTH
    cos_in, sin_in = (np.cos(inner), np.sin(inner))
    twist = 2.0 * np.pi * np.outer(quarter, np.arange(WIDTH)) / LENGTH
    low = lambda array: array.astype(np.float32).astype(jnp.bfloat16)
    return dict(
        first=low(first),
        first_by_channel=low(first[:, by_channel]),
        middle=low(np.concatenate([cos_in, sin_in], 1)),
        last=low(last),
        last_by_channel=low(last[by_channel]),
        twist=np.stack([np.cos(twist), np.sin(twist)]).astype(np.float32),
    )


def dot(left, right, dims=((1,), (0,))):
    return lax.dot_general(
        left.astype(jnp.bfloat16),
        right.astype(jnp.bfloat16),
        (dims, ((), ())),
        preferred_element_type=jnp.float32,
    )


def source_of(half, row, place):
    return jnp.where(row == 0, 8 * half + (place & 7), (place - row - 8 * half) & 15)


def order_of(place):
    row = lax.broadcasted_iota(jnp.int32, (WIDTH, WIDTH), 0)
    channel = lax.broadcasted_iota(jnp.int32, (WIDTH, WIDTH), 1)
    wanted = 16 * source_of(row >> 7, row & 7, place) + ((row >> 3) & 15)
    return (channel == wanted).astype(jnp.float32).astype(jnp.bfloat16)


def whirl(both, middle, twist_first, twist):
    if twist_first:
        both = twisted(both, twist)
    terms = dot(both, middle)
    real, imag = (terms[:WIDTH], terms[WIDTH:])
    both = jnp.concatenate(
        [real[:, :WIDTH] + imag[:, WIDTH:], imag[:, :WIDTH] - real[:, WIDTH:]], 0
    )
    return both if twist_first else twisted(both, twist)


def twisted(both, twist):
    shape = (BLOCKS, MINE, WIDTH)
    cos, sin = (twist[0][:, None, :], twist[1][:, None, :])
    real, imag = (both[:WIDTH].reshape(shape), both[WIDTH:].reshape(shape))
    both = jnp.concatenate([real * cos + imag * sin, imag * cos - real * sin], 0)
    return both.reshape(2 * WIDTH, WIDTH)


def forward(rows, first, middle, twist):
    return whirl(dot(first, rows), middle, True, twist)


def inverse(real, imag, middle, last, twist):
    return dot(last, whirl(jnp.concatenate([real, imag], 0), middle, False, twist))


def parts_of(spectrum):
    return (spectrum[:WIDTH], spectrum[WIDTH:])


def pack(upper, lower, extra):
    pieces = []
    for rows in (upper, lower):
        rows = rows.reshape(BLOCKS, MINE, WIDTH)
        pieces += [rows[:, :, :128], rows[:, :, 128:]]
    shape = (BLOCKS, MINE // 2, 128)
    for piece in (extra[:, :128], extra[:, 128:]):
        pieces.append(jnp.broadcast_to(piece[:, None, :], shape))
    return jnp.concatenate(pieces, 1).astype(jnp.bfloat16)


def rows_of(block, at):
    block = block.astype(jnp.float32)
    left = block[:, at : at + MINE].reshape(BLOCKS * MINE, 128)
    right = block[:, at + MINE : at + 2 * MINE].reshape(BLOCKS * MINE, 128)
    return jnp.concatenate([left, right], 1)


def extra_of(block):
    block = block[:, 4 * MINE :].astype(jnp.float32)
    return jnp.concatenate([block[:, 0], block[:, MINE // 2]], 1)


def product_of(cotangent, gates):
    return (cotangent.astype(jnp.float32) * gates.astype(jnp.float32)).astype(jnp.bfloat16)


def outgoing(place, values, gates, cotangent, filters):
    gated = product_of(cotangent, gates)
    across = ((1,), (1,))
    order = order_of(place)
    twice = jnp.concatenate([filters, filters], 0).astype(jnp.float32)
    return pack(dot(order, values, across), dot(order, gated, across), twice)


def spectra(block, first, middle, last_by_channel, twist):
    value = forward(rows_of(block, 0), first, middle, twist)
    gated = forward(rows_of(block, 2 * MINE), first, middle, twist)
    (value_r, value_i), (gated_r, gated_i) = (parts_of(value), parts_of(gated))
    lagged = inverse(
        gated_r * value_r + gated_i * value_i,
        gated_r * value_i - gated_i * value_r,
        middle, last_by_channel, twist,
    ) * (1.0 / LENGTH)
    lagged = lagged.reshape(MINE, BLOCKS, WIDTH)
    return (value, gated, lagged.astype(jnp.bfloat16), extra_of(block).astype(jnp.bfloat16))


def results(filters, total, value, gated, first_by_channel, middle, last, twist):
    filt = forward(filters.reshape(MINE * BLOCKS, WIDTH), first_by_channel, middle, twist)
    (filt_r, filt_i) = parts_of(filt)
    (value_r, value_i), (gated_r, gated_i) = (parts_of(value), parts_of(gated))
    scale = FACTOR / LENGTH
    conv = inverse(
        filt_r * value_r - filt_i * value_i,
        -filt_r * value_i - filt_i * value_r,
        middle, last, twist,
    ) * scale
    back = inverse(
        filt_r * gated_r + filt_i * gated_i,
        filt_i * gated_r - filt_r * gated_i,
        middle, last, twist,
    ) * scale
    return pack(conv, back, total * FACTOR)


def finished(place, block, values, gates, cotangent, skip_rows):
    down = ((0,), (0,))
    order = order_of(place)
    conv = dot(rows_of(block, 0), order, down)
    back = dot(rows_of(block, 2 * MINE), order, down)
    gated = product_of(cotangent, gates).astype(jnp.float32)
    grad_gates = cotangent.astype(jnp.float32) * (conv + skip_rows[:1] * values.astype(jnp.float32))
    grad_values = back + skip_rows[:1] * gated
    partial = extra_of(block)
    grad_filters = partial[:HALF] + partial[HALF:]
    return tuple(out.astype(jnp.bfloat16) for out in (grad_gates, grad_values, grad_filters))


def outgoing_kernel(mp_place, values, gates, cotangent, filters, out, *scratch):
    held, sems = (scratch[:-1], scratch[-1])
    copies = []
    for at, (source, target) in enumerate(zip((values, gates, cotangent, filters), held)):
        copies.append(pltpu.make_async_copy(source, target, sems.at[at]))
        copies[-1].start()
    for copy in copies:
        copy.wait()
    out[...] = outgoing(mp_place[0], *(ref[...] for ref in held))


def spectra_kernel(ctx_half, mp_place, *refs):
    half, place = (ctx_half[0], mp_place[0])
    value, gated, own, sent = refs[-4:]
    value[...], gated[...], lagged, own_rows = spectra(*(ref[...] for ref in refs[:-4]))
    own[...] = own_rows
    sent[...] = jnp.broadcast_to(own_rows[None], sent.shape)
    for row in range(MINE):
        sent[source_of(half, row, place)] = lagged[row]


def results_kernel(ctx_half, mp_place, arrived, own, *refs):
    half, place = (ctx_half[0], mp_place[0])
    held = source_of(half, 0, place) == place
    filters = [jnp.where(held, own[...], arrived[source_of(half, 0, place)])]
    filters += [arrived[source_of(half, row, place)] for row in range(1, MINE)]
    total = jnp.zeros((BLOCKS, WIDTH), jnp.float32)
    for other in range(SHARDS):
        ahead = (other - place) & 15
        near = (ahead >= 1) & (ahead <= 7) | (place == other & 7)
        total += jnp.where(near == (half == 0), arrived[other].astype(jnp.float32), 0.0)
    refs[-1][...] = results(jnp.stack(filters), total, *(ref[...] for ref in refs[:-1]))


def finished_kernel(mp_place, *refs):
    outs = finished(mp_place[0], *(ref[...] for ref in refs[:-3]))
    for ref, out in zip(refs[-3:], outs):
        ref[...] = out


def call(kernel, outs, args, flops, scalars=0, fetched=False):
    whole = pl.BlockSpec(memory_space=pltpu.VMEM)
    scalar = pl.BlockSpec(memory_space=pltpu.SMEM)
    given = pl.BlockSpec(memory_space=pl.ANY) if fetched else whole
    size = sum(math.prod(out.shape) * out.dtype.itemsize for out in (*outs, *args))
    single = len(outs) == 1
    scratch = []
    if fetched:
        scratch = [pltpu.VMEM(arg.shape, arg.dtype) for arg in args[scalars:]]
        scratch.append(pltpu.SemaphoreType.DMA((len(scratch),)))
    return pl.pallas_call(
        kernel,
        out_shape=outs[0] if single else outs,
        in_specs=[scalar] * scalars + [given] * (len(args) - scalars),
        out_specs=whole if single else (whole,) * len(outs),
        scratch_shapes=scratch,
        compiler_params=pltpu.CompilerParams(vmem_limit_bytes=MOST if fetched else VMEM),
        cost_estimate=pl.CostEstimate(flops=flops, bytes_accessed=size, transcendentals=0),
    )(*args)


def swap(block, axis):
    return lax.all_to_all(block, axis, split_axis=0, concat_axis=0, tiled=True)


def per_device(table, values, gates, cotangent, filters, skip_gain):
    shape = functools.partial(jax.ShapeDtypeStruct, dtype=jnp.bfloat16)
    spectrum = jax.ShapeDtypeStruct((2 * WIDTH, WIDTH), jnp.float32)
    packed = shape((BLOCKS, 5 * MINE, 128))
    ctx_half = (lax.axis_index("ctx") // HALF).astype(jnp.int32).reshape(1)
    mp_place = lax.axis_index("mp").astype(jnp.int32).reshape(1)
    skip_rows = jnp.broadcast_to(skip_gain[None, :], (8, WIDTH))
    cube = 2 * WIDTH**3

    block = call(
        outgoing_kernel, (packed,), (mp_place, values, gates, cotangent, filters.T),
        2 * cube, scalars=1, fetched=True,
    )
    block = swap(block, "ctx")
    value, gated, own, sent = call(
        spectra_kernel,
        (spectrum, spectrum, shape((BLOCKS, WIDTH)), shape((SHARDS, BLOCKS, WIDTH))),
        (ctx_half, mp_place, block, table["first"], table["middle"], table["last_by_channel"], table["twist"]),
        18 * cube, scalars=2,
    )
    sent = swap(sent, "mp")
    block = call(
        results_kernel, (packed,),
        (ctx_half, mp_place, sent, own, value, gated, table["first_by_channel"], table["middle"], table["last"], table["twist"]),
        18 * cube, scalars=2,
    )
    block = swap(block, "ctx")
    grad_gates, grad_values, grad_filters = call(
        finished_kernel, (shape(values.shape), shape(values.shape), shape((HALF, WIDTH))),
        (mp_place, block, values, gates, cotangent, skip_rows), 2 * cube, scalars=1,
    )
    return (grad_gates, grad_values, grad_filters.T)


def solution(mesh):
    return jax.shard_map(
        functools.partial(per_device, tables()),
        mesh=mesh,
        in_specs=(P("ctx", "mp"), P("ctx", "mp"), P("ctx", "mp"), P("ctx", "mp"), P("mp")),
        out_specs=(P("ctx", "mp"), P("ctx", "mp"), P("ctx", "mp")),
        check_vma=False,
    )
```

time: 101 us -> 91.4 us (0.905)
  waiting for transfers between devices: 33.3 us -> 22.5 us
  local copies, waits for them, and re-layouts: 6.01 us -> 0.07 us
  blocking collectives: 39.4 us -> 43.7 us
  starting transfers between devices: 13.9 us -> 17.1 us
    all_to_all x2 -> x1, waiting for transfers between devices: 33.3 us -> 22.5 us  [swap(): return lax.all_to_all(block, axis, split_axis=0, concat_axis=0, tiled=True)]
    unnamed x30 -> x20, local copies, waits for them, and re-layouts: 6.01 us -> 0.07 us
    all_to_all x1 -> x2, blocking collectives: 39.4 us -> 43.7 us  [swap(): return lax.all_to_all(block, axis, split_axis=0, concat_axis=0, tiled=True)]
    all_to_all x2 -> x1, starting transfers between devices: 13.9 us -> 17.1 us  [swap(): return lax.all_to_all(block, axis, split_axis=0, concat_axis=0, tiled=True)]
  transfers between devices with their start and end apart: 2 -> 1, of which waited for: 2 -> 1; matrix products, arithmetic and copies ran while one was open for 0% -> 0% of each run, Pallas kernels for 0% -> 0%
where the time goes in v3:
time: 91.4 us; the launch traced here: 90 us
  blocking collectives  43.7 us (48%)
  waiting for transfers between devices  22.5 us (25%)
  starting transfers between devices  17.1 us (19%)
  Pallas kernels  5.87 us (6%)
    all_to_all x2, blocking collectives, swap(): return lax.all_to_all(block, axis, split_axis=0, concat_axis=0, tiled=True)  43.7 us
    all_to_all x1, waiting for transfers between devices, swap(): return lax.all_to_all(block, axis, split_axis=0, concat_axis=0, tiled=True)  22.5 us
    all_to_all x1, starting transfers between devices, swap(): return lax.all_to_all(block, axis, split_axis=0, concat_axis=0, tiled=True)  17.1 us
    pallas_call x4, Pallas kernels, call(): pl.pallas_call(kernel, out_shape=outs[0] if single else outs, in_specs=[s...  5.87 us
  transfers between devices with their start and end apart: 1, of which 1 were waited for; matrix products, arithmetic and copies ran while one was open for 0% of the time, Pallas kernels for 0%

profile of v3, /device:TPU:1, one launch (start us, length us, event | category | flops | bytes accessed | tf_op | source)
XLA Modules:
  0.0 90.0 jit_solution(12172196145676810603)
XLA Ops:
  0.6 0.0 copy-start.8
  0.6 2.1 %shard_map.130 = bf16[32,40,128]{2,1,0:T(8,128)(2,1)} custom-call(s32[1]{0:T(128)} %bitcast.mp_place, bf16[256,256]{1,0:T(8,128)(2,1)} %refs_1_.2, bf16[256,256]{1,0:T(8,128)(2,1)} %refs_2_.3, bf16[256,256]{1,0:T(8,128)(2,1)} %refs_3_.3, bf16[16,256]{1,0:T(8,128)(2,1)} %bitcast.4), custom_call_target="tpu_custom_call" | custom-call | flops 67108864 | bytes 729092 | tf_op jit(solution)/shard_map/pallas_call | solution.py:226
  2.8 0.0 copy-start.3
  2.8 0.0 copy-start.6
  2.8 0.0 copy-start.7
  2.8 17.1 %all-to-all-start = ((bf16[32,40,128]{2,1,0:T(8,128)(2,1)}), bf16[32,40,128]{2,1,0:T(8,128)(2,1)S(1)}, u32[]{:S(2)}, u32[]{:S(2)}) async-start(bf16[32,40,128]{2,1,0:T(8,128)(2,1)} %shard_map.130), calls=%async_computation | async-start | bytes 655360 | tf_op jit(solution)/shard_map/all_to_all | solution.py:238
  19.9 22.5 %all-to-all-done.refs_0_ = bf16[32,40,128]{2,1,0:T(8,128)(2,1)S(1)} async-done(((bf16[32,40,128]{2,1,0:T(8,128)(2,1)}), bf16[32,40,128]{2,1,0:T(8,128)(2,1)S(1)}, u32[]{:S(2)}, u32[]{:S(2)}) %all-to-all-start) | async-done | bytes 327712 | tf_op jit(solution)/shard_map/all_to_all | solution.py:238
  42.4 0.0 copy-done.8
  42.4 0.0 copy-done.3
  42.4 0.0 copy-done.6
  42.4 0.0 copy-done.7
  42.4 1.3 %shard_map.131 = (f32[512,256]{1,0:T(8,128)S(1)}, f32[512,256]{1,0:T(8,128)S(1)}, bf16[32,256]{1,0:T(8,128)(2,1)S(1)}, bf16[16,32,256]{2,1,0:T(8,128)(2,1)S(1)}) custom-call(s32[1]{0:T(128)} %bitcast.1.ctx_half, s32[1]{0:T(128)} %bitcast.mp_place, bf16[32,40,128]{2,1,0:T(8,128)(2,1)S(1)} %all-to-all-done.refs_0_, bf16[512,256]{1,0:T(8,128)(2,1)S(1)} %copy-done.7, ...), custom_call_target="tpu_custom_call" | custom-call | flops 603979776 | bytes 2506760 | tf_op jit(solution)/shard_map/pallas_call | solution.py:226
  43.7 0.0 copy-start.4
  43.7 0.0 copy-start.5
  43.7 18.4 %all_to_all.15.arrived = bf16[16,32,256]{2,1,0:T(8,128)(2,1)S(1)} all-to-all(bf16[16,32,256]{2,1,0:T(8,128)(2,1)S(1)} %get-tuple-element.10), channel_id=1, replica_groups=mesh['ctx'=32,'mp'=16] {'mp'}, dimensions={0} | all-to-all | bytes 524288 | tf_op jit(solution)/shard_map/all_to_all | solution.py:238
  62.1 0.0 copy-done.4
  62.2 1.5 %shard_map.132 = bf16[32,40,128]{2,1,0:T(8,128)(2,1)S(1)} custom-call(s32[1]{0:T(128)} %bitcast.1.ctx_half, s32[1]{0:T(128)} %bitcast.mp_place, bf16[16,32,256]{2,1,0:T(8,128)(2,1)S(1)} %all_to_all.15.arrived, bf16[32,256]{1,0:T(8,128)(2,1)S(1)} %get-tuple-element.11.own, f32[512,256]{1,0:T(8,128)S(1)} %get-tuple-element.12.refs_0_, ...), custom_call_target="tpu_custom_call" | custom-call | flops 603979776 | bytes 2506760 | tf_op jit(solution)/shard_map/pallas_call | solution.py:226
  63.6 0.0 copy-start.9
  63.7 0.0 copy-start
  63.7 0.0 copy-start.1
  63.7 0.0 copy-start.2
  63.7 25.3 %all_to_all.16.refs_0_ = bf16[32,40,128]{2,1,0:T(8,128)(2,1)S(1)} all-to-all(bf16[32,40,128]{2,1,0:T(8,128)(2,1)S(1)} %shard_map.132), channel_id=1, replica_groups=mesh['ctx'=32,'mp'=16] {'ctx'}, dimensions={0} | all-to-all | bytes 655360 | tf_op jit(solution)/shard_map/all_to_all | solution.py:238
  89.0 0.0 copy-done
  89.0 1.0 %shard_map.133 = (bf16[256,256]{1,0:T(8,128)(2,1)}, bf16[256,256]{1,0:T(8,128)(2,1)}, bf16[16,256]{1,0:T(8,128)(2,1)}) custom-call(s32[1]{0:T(128)} %bitcast.mp_place, bf16[32,40,128]{2,1,0:T(8,128)(2,1)S(1)} %all_to_all.16.refs_0_, bf16[256,256]{1,0:T(8,128)(2,1)S(1)} %copy-done, bf16[256,256]{1,0:T(8,128)(2,1)S(1)} %copy-done.1, ...), custom_call_target="tpu_custom_call" | custom-call | flops 67108864 | bytes 999428 | tf_op jit(solution)/shard_map/pallas_call | solution.py:226
  (5 shorter events, 0.0 us)
Async XLA Ops:
  0.6 41.8 %copy-start.8 = (bf16[256,512]{1,0:T(8,128)(2,1)S(1)}, bf16[256,512]{1,0:T(8,128)(2,1)}, u32[]{:S(2)}) copy-start(bf16[256,512]{1,0:T(8,128)(2,1)} %constant.39.clone.refs_3_) | copy-start | bytes 786436
  2.8 39.7 %copy-start.3 = (bf16[256,512]{1,0:T(8,128)(2,1)S(1)}, bf16[256,512]{1,0:T(8,128)(2,1)}, u32[]{:S(2)}) copy-start(bf16[256,512]{1,0:T(8,128)(2,1)} %constant.38.clone.refs_2_.refs_3_) | copy-start | bytes 786436
  2.8 39.6 %copy-start.6 = (f32[2,32,256]{2,1,0:T(8,128)S(1)}, f32[2,32,256]{2,1,0:T(8,128)}, u32[]{:S(2)}) copy-start(f32[2,32,256]{2,1,0:T(8,128)} %constant.40.clone.refs_4_.refs_5_) | copy-start | bytes 196612
  2.8 39.6 %copy-start.7 = (bf16[512,256]{1,0:T(8,128)(2,1)S(1)}, bf16[512,256]{1,0:T(8,128)(2,1)}, u32[]{:S(2)}) copy-start(bf16[512,256]{1,0:T(8,128)(2,1)} %constant.37.clone.refs_1_) | copy-start | bytes 786436
  2.8 39.6 %all-to-all-start = ((bf16[32,40,128]{2,1,0:T(8,128)(2,1)}), bf16[32,40,128]{2,1,0:T(8,128)(2,1)S(1)}, u32[]{:S(2)}, u32[]{:S(2)}) async-start(bf16[32,40,128]{2,1,0:T(8,128)(2,1)} %shard_map.130), calls=%async_computation | async-start | bytes 655360 | tf_op jit(solution)/shard_map/all_to_all | solution.py:238
  43.7 18.4 %copy-start.4 = (bf16[512,256]{1,0:T(8,128)(2,1)S(1)}, bf16[512,256]{1,0:T(8,128)(2,1)}, u32[]{:S(2)}) copy-start(bf16[512,256]{1,0:T(8,128)(2,1)} %constant.41.clone.refs_2_) | copy-start | bytes 786436
  43.7 18.4 %copy-start.5 = (bf16[256,512]{1,0:T(8,128)(2,1)S(1)}, bf16[256,512]{1,0:T(8,128)(2,1)}, u32[]{:S(2)}) copy-start(bf16[256,512]{1,0:T(8,128)(2,1)} %constant.42.clone.refs_4_) | copy-start | bytes 786436
  63.6 25.3 %copy-start.9 = (f32[256]{0:T(256)S(1)}, f32[256]{0:T(256)}, u32[]{:S(2)}) copy-start(f32[256]{0:T(256)} %param.15) | copy-start | bytes 3076
  63.7 25.3 %copy-start = (bf16[256,256]{1,0:T(8,128)(2,1)S(1)}, bf16[256,256]{1,0:T(8,128)(2,1)}, u32[]{:S(2)}) copy-start(bf16[256,256]{1,0:T(8,128)(2,1)} %refs_1_.2) | copy-start | bytes 393220
  63.7 25.3 %copy-start.1 = (bf16[256,256]{1,0:T(8,128)(2,1)S(1)}, bf16[256,256]{1,0:T(8,128)(2,1)}, u32[]{:S(2)}) copy-start(bf16[256,256]{1,0:T(8,128)(2,1)} %refs_2_.3) | copy-start | bytes 393220
  63.7 25.3 %copy-start.2 = (bf16[256,256]{1,0:T(8,128)(2,1)S(1)}, bf16[256,256]{1,0:T(8,128)(2,1)}, u32[]{:S(2)}) copy-start(bf16[256,256]{1,0:T(8,128)(2,1)} %refs_3_.3) | copy-start | bytes 393220

commit v4 on v3

--- a/solution.py
+++ b/solution.py
@@ -98,40 +98,38 @@
     pieces = []
     for rows in (upper, lower):
         rows = rows.reshape(BLOCKS, MINE, WIDTH)
-        pieces += [rows[:, :, :128], rows[:, :, 128:]]
-    shape = (BLOCKS, MINE // 2, 128)
-    for piece in (extra[:, :128], extra[:, 128:]):
-        pieces.append(jnp.broadcast_to(piece[:, None, :], shape))
-    return jnp.concatenate(pieces, 1).astype(jnp.bfloat16)
+        pieces += [rows[:, at : at + 2, :] for at in range(0, MINE, 2)]
+    spread = [piece[:, None, :] for piece in (extra[:, :128], extra[:, 128:])]
+    pieces.append(jnp.concatenate(spread, 1))
+    return jnp.concatenate(pieces, 2).astype(jnp.bfloat16)
 
 
 def rows_of(block, at):
-    block = block.astype(jnp.float32)
-    left = block[:, at : at + MINE].reshape(BLOCKS * MINE, 128)
-    right = block[:, at + MINE : at + 2 * MINE].reshape(BLOCKS * MINE, 128)
-    return jnp.concatenate([left, right], 1)
+    start = 4 * WIDTH * at
+    block = block[:, :, start : start + 4 * WIDTH].astype(jnp.float32)
+    rows = jnp.concatenate([block[:, :, k * WIDTH : (k + 1) * WIDTH] for k in range(4)], 1)
+    return rows.reshape(BLOCKS * MINE, WIDTH)
 
 
 def extra_of(block):
-    block = block[:, 4 * MINE :].astype(jnp.float32)
-    return jnp.concatenate([block[:, 0], block[:, MINE // 2]], 1)
+    block = block[:, :, 8 * WIDTH :].astype(jnp.float32)
+    return jnp.concatenate([block[:, 0], block[:, 1]], 1)
 
 
 def product_of(cotangent, gates):
     return (cotangent.astype(jnp.float32) * gates.astype(jnp.float32)).astype(jnp.bfloat16)
 
 
-def outgoing(place, values, gates, cotangent, filters):
+def outgoing(order, values, gates, cotangent, filters):
     gated = product_of(cotangent, gates)
     across = ((1,), (1,))
-    order = order_of(place)
     twice = jnp.concatenate([filters, filters], 0).astype(jnp.float32)
     return pack(dot(order, values, across), dot(order, gated, across), twice)
 
 
 def spectra(block, first, middle, last_by_channel, twist):
     value = forward(rows_of(block, 0), first, middle, twist)
-    gated = forward(rows_of(block, 2 * MINE), first, middle, twist)
+    gated = forward(rows_of(block, 1), first, middle, twist)
     (value_r, value_i), (gated_r, gated_i) = (parts_of(value), parts_of(gated))
     lagged = inverse(
         gated_r * value_r + gated_i * value_i,
@@ -164,7 +162,7 @@
     down = ((0,), (0,))
     order = order_of(place)
     conv = dot(rows_of(block, 0), order, down)
-    back = dot(rows_of(block, 2 * MINE), order, down)
+    back = dot(rows_of(block, 1), order, down)
     gated = product_of(cotangent, gates).astype(jnp.float32)
     grad_gates = cotangent.astype(jnp.float32) * (conv + skip_rows[:1] * values.astype(jnp.float32))
     grad_values = back + skip_rows[:1] * gated
@@ -179,9 +177,10 @@
     for at, (source, target) in enumerate(zip((values, gates, cotangent, filters), held)):
         copies.append(pltpu.make_async_copy(source, target, sems.at[at]))
         copies[-1].start()
+    order = order_of(mp_place[0])
     for copy in copies:
         copy.wait()
-    out[...] = outgoing(mp_place[0], *(ref[...] for ref in held))
+    out[...] = outgoing(order, *(ref[...] for ref in held))
 
 
 def spectra_kernel(ctx_half, mp_place, *refs):
@@ -241,7 +240,7 @@
 def per_device(table, values, gates, cotangent, filters, skip_gain):
     shape = functools.partial(jax.ShapeDtypeStruct, dtype=jnp.bfloat16)
     spectrum = jax.ShapeDtypeStruct((2 * WIDTH, WIDTH), jnp.float32)
-    packed = shape((BLOCKS, 5 * MINE, 128))
+    packed = shape((BLOCKS, 2, 8 * WIDTH + 128))
     ctx_half = (lax.axis_index("ctx") // HALF).astype(jnp.int32).reshape(1)
     mp_place = lax.axis_index("mp").astype(jnp.int32).reshape(1)
     skip_rows = jnp.broadcast_to(skip_gain[None, :], (8, WIDTH))

time: 91.4 us -> 87.6 us (0.958)
  blocking collectives: 43.7 us -> 41.5 us
  waiting for transfers between devices: 22.5 us -> 20.5 us
    all_to_all x2, blocking collectives: 43.7 us -> 41.5 us  [swap(): return lax.all_to_all(block, axis, split_axis=0, concat_axis=0, tiled=True)]
    all_to_all x1, waiting for transfers between devices: 22.5 us -> 20.5 us  [swap(): return lax.all_to_all(block, axis, split_axis=0, concat_axis=0, tiled=True)]
where the time goes in v4:
time: 87.6 us; the launch traced here: 86.1 us
  blocking collectives  41.5 us (47%)
  waiting for transfers between devices  20.5 us (23%)
  starting transfers between devices  17.1 us (20%)
  Pallas kernels  6.16 us (7%)
    all_to_all x2, blocking collectives, swap(): return lax.all_to_all(block, axis, split_axis=0, concat_axis=0, tiled=True)  41.5 us
    all_to_all x1, waiting for transfers between devices, swap(): return lax.all_to_all(block, axis, split_axis=0, concat_axis=0, tiled=True)  20.5 us
    all_to_all x1, starting transfers between devices, swap(): return lax.all_to_all(block, axis, split_axis=0, concat_axis=0, tiled=True)  17.1 us
    pallas_call x4, Pallas kernels, call(): pl.pallas_call(kernel, out_shape=outs[0] if single else outs, in_specs=[s...  6.16 us
  transfers between devices with their start and end apart: 1, of which 1 were waited for; matrix products, arithmetic and copies ran while one was open for 0% of the time, Pallas kernels for 0%

profile of v4, /device:TPU:1, one launch (start us, length us, event | category | flops | bytes accessed | tf_op | source)
XLA Modules:
  0.0 86.1 jit_solution(11547849170063814657)
XLA Ops:
  0.6 0.0 copy-start.8
  0.6 2.2 %shard_map.130 = bf16[32,2,2176]{2,1,0:T(2,128)(2,1)} custom-call(s32[1]{0:T(128)} %bitcast.mp_place, bf16[256,256]{1,0:T(8,128)(2,1)} %refs_1_.2, bf16[256,256]{1,0:T(8,128)(2,1)} %refs_2_.3, bf16[256,256]{1,0:T(8,128)(2,1)} %refs_3_.3, bf16[16,256]{1,0:T(8,128)(2,1)} %bitcast.4), custom_call_target="tpu_custom_call" | custom-call | flops 67108864 | bytes 679940 | tf_op jit(solution)/shard_map/pallas_call | solution.py:225
  2.9 0.0 copy-start.3
  2.9 0.0 copy-start.6
  2.9 0.0 copy-start.7
  2.9 17.1 %all-to-all-start = ((bf16[32,2,2176]{2,1,0:T(2,128)(2,1)}), bf16[32,2,2176]{2,1,0:T(2,128)(2,1)S(1)}, u32[]{:S(2)}, u32[]{:S(2)}) async-start(bf16[32,2,2176]{2,1,0:T(2,128)(2,1)} %shard_map.130), calls=%async_computation | async-start | bytes 557056 | tf_op jit(solution)/shard_map/all_to_all | solution.py:237
  20.0 20.5 %all-to-all-done.refs_0_ = bf16[32,2,2176]{2,1,0:T(2,128)(2,1)S(1)} async-done(((bf16[32,2,2176]{2,1,0:T(2,128)(2,1)}), bf16[32,2,2176]{2,1,0:T(2,128)(2,1)S(1)}, u32[]{:S(2)}, u32[]{:S(2)}) %all-to-all-start) | async-done | bytes 278560 | tf_op jit(solution)/shard_map/all_to_all | solution.py:237
  40.5 0.0 copy-done.8
  40.5 0.0 copy-done.3
  40.5 0.0 copy-done.6
  40.5 0.0 copy-done.7
  40.5 1.3 %shard_map.131 = (f32[512,256]{1,0:T(8,128)S(1)}, f32[512,256]{1,0:T(8,128)S(1)}, bf16[32,256]{1,0:T(8,128)(2,1)S(1)}, bf16[16,32,256]{2,1,0:T(8,128)(2,1)S(1)}) custom-call(s32[1]{0:T(128)} %bitcast.1.ctx_half, s32[1]{0:T(128)} %bitcast.mp_place, bf16[32,2,2176]{2,1,0:T(2,128)(2,1)S(1)} %all-to-all-done.refs_0_, bf16[512,256]{1,0:T(8,128)(2,1)S(1)} %copy-done.7, ...), custom_call_target="tpu_custom_call" | custom-call | flops 603979776 | bytes 2457608 | tf_op jit(solution)/shard_map/pallas_call | solution.py:225
  41.8 0.0 copy-start.4
  41.9 0.0 copy-start.5
  41.9 18.2 %all_to_all.15.arrived = bf16[16,32,256]{2,1,0:T(8,128)(2,1)S(1)} all-to-all(bf16[16,32,256]{2,1,0:T(8,128)(2,1)S(1)} %get-tuple-element.10), channel_id=1, replica_groups=mesh['ctx'=32,'mp'=16] {'mp'}, dimensions={0} | all-to-all | bytes 524288 | tf_op jit(solution)/shard_map/all_to_all | solution.py:237
  60.0 0.0 copy-done.4
  60.1 1.6 %shard_map.132 = bf16[32,2,2176]{2,1,0:T(2,128)(2,1)S(1)} custom-call(s32[1]{0:T(128)} %bitcast.1.ctx_half, s32[1]{0:T(128)} %bitcast.mp_place, bf16[16,32,256]{2,1,0:T(8,128)(2,1)S(1)} %all_to_all.15.arrived, bf16[32,256]{1,0:T(8,128)(2,1)S(1)} %get-tuple-element.11.own, f32[512,256]{1,0:T(8,128)S(1)} %get-tuple-element.12.refs_0_, ...), custom_call_target="tpu_custom_call" | custom-call | flops 603979776 | bytes 2457608 | tf_op jit(solution)/shard_map/pallas_call | solution.py:225
  61.6 0.0 copy-start.9
  61.6 0.0 copy-start
  61.7 0.0 copy-start.1
  61.7 0.0 copy-start.2
  61.7 23.3 %all_to_all.16.refs_0_ = bf16[32,2,2176]{2,1,0:T(2,128)(2,1)S(1)} all-to-all(bf16[32,2,2176]{2,1,0:T(2,128)(2,1)S(1)} %shard_map.132), channel_id=1, replica_groups=mesh['ctx'=32,'mp'=16] {'ctx'}, dimensions={0} | all-to-all | bytes 557056 | tf_op jit(solution)/shard_map/all_to_all | solution.py:237
  85.0 0.0 copy-done.1
  85.0 1.1 %shard_map.133 = (bf16[256,256]{1,0:T(8,128)(2,1)}, bf16[256,256]{1,0:T(8,128)(2,1)}, bf16[16,256]{1,0:T(8,128)(2,1)}) custom-call(s32[1]{0:T(128)} %bitcast.mp_place, bf16[32,2,2176]{2,1,0:T(2,128)(2,1)S(1)} %all_to_all.16.refs_0_, bf16[256,256]{1,0:T(8,128)(2,1)S(1)} %copy-done, bf16[256,256]{1,0:T(8,128)(2,1)S(1)} %copy-done.1, ...), custom_call_target="tpu_custom_call" | custom-call | flops 67108864 | bytes 950276 | tf_op jit(solution)/shard_map/pallas_call | solution.py:225
  (5 shorter events, 0.0 us)
Async XLA Ops:
  0.6 39.9 %copy-start.8 = (bf16[256,512]{1,0:T(8,128)(2,1)S(1)}, bf16[256,512]{1,0:T(8,128)(2,1)}, u32[]{:S(2)}) copy-start(bf16[256,512]{1,0:T(8,128)(2,1)} %constant.39.clone.refs_3_) | copy-start | bytes 786436
  2.9 37.7 %copy-start.3 = (bf16[256,512]{1,0:T(8,128)(2,1)S(1)}, bf16[256,512]{1,0:T(8,128)(2,1)}, u32[]{:S(2)}) copy-start(bf16[256,512]{1,0:T(8,128)(2,1)} %constant.38.clone.refs_2_.refs_3_) | copy-start | bytes 786436
  2.9 37.6 %copy-start.6 = (f32[2,32,256]{2,1,0:T(8,128)S(1)}, f32[2,32,256]{2,1,0:T(8,128)}, u32[]{:S(2)}) copy-start(f32[2,32,256]{2,1,0:T(8,128)} %constant.40.clone.refs_4_.refs_5_) | copy-start | bytes 196612
  2.9 37.6 %copy-start.7 = (bf16[512,256]{1,0:T(8,128)(2,1)S(1)}, bf16[512,256]{1,0:T(8,128)(2,1)}, u32[]{:S(2)}) copy-start(bf16[512,256]{1,0:T(8,128)(2,1)} %constant.37.clone.refs_1_) | copy-start | bytes 786436
  2.9 37.6 %all-to-all-start = ((bf16[32,2,2176]{2,1,0:T(2,128)(2,1)}), bf16[32,2,2176]{2,1,0:T(2,128)(2,1)S(1)}, u32[]{:S(2)}, u32[]{:S(2)}) async-start(bf16[32,2,2176]{2,1,0:T(2,128)(2,1)} %shard_map.130), calls=%async_computation | async-start | bytes 557056 | tf_op jit(solution)/shard_map/all_to_all | solution.py:237
  41.8 18.2 %copy-start.4 = (bf16[512,256]{1,0:T(8,128)(2,1)S(1)}, bf16[512,256]{1,0:T(8,128)(2,1)}, u32[]{:S(2)}) copy-start(bf16[512,256]{1,0:T(8,128)(2,1)} %constant.41.clone.refs_2_) | copy-start | bytes 786436
  41.9 18.2 %copy-start.5 = (bf16[256,512]{1,0:T(8,128)(2,1)S(1)}, bf16[256,512]{1,0:T(8,128)(2,1)}, u32[]{:S(2)}) copy-start(bf16[256,512]{1,0:T(8,128)(2,1)} %constant.42.clone.refs_4_) | copy-start | bytes 786436
  61.6 23.4 %copy-start.9 = (f32[256]{0:T(256)S(1)}, f32[256]{0:T(256)}, u32[]{:S(2)}) copy-start(f32[256]{0:T(256)} %param.15) | copy-start | bytes 3076
  61.6 23.4 %copy-start = (bf16[256,256]{1,0:T(8,128)(2,1)S(1)}, bf16[256,256]{1,0:T(8,128)(2,1)}, u32[]{:S(2)}) copy-start(bf16[256,256]{1,0:T(8,128)(2,1)} %refs_1_.2) | copy-start | bytes 393220
  61.7 23.4 %copy-start.1 = (bf16[256,256]{1,0:T(8,128)(2,1)S(1)}, bf16[256,256]{1,0:T(8,128)(2,1)}, u32[]{:S(2)}) copy-start(bf16[256,256]{1,0:T(8,128)(2,1)} %refs_2_.3) | copy-start | bytes 393220
  61.7 23.4 %copy-start.2 = (bf16[256,256]{1,0:T(8,128)(2,1)S(1)}, bf16[256,256]{1,0:T(8,128)(2,1)}, u32[]{:S(2)}) copy-start(bf16[256,256]{1,0:T(8,128)(2,1)} %refs_3_.3) | copy-start | bytes 393220

commit v5 on v4

--- a/solution.py
+++ b/solution.py
@@ -17,7 +17,6 @@
 SHARDS = 16
 FACTOR = 1.0 / math.sqrt(LENGTH)
 VMEM = 32 * 1024 * 1024
-MOST = 63 * 1024 * 1024
 
 
 def tables():
@@ -36,7 +35,7 @@
     return dict(
         first=low(first),
         first_by_channel=low(first[:, by_channel]),
-        middle=low(np.concatenate([cos_in, sin_in], 1)),
+        middle=low(np.block([[cos_in, -sin_in], [sin_in, cos_in]])),
         last=low(last),
         last_by_channel=low(last[by_channel]),
         twist=np.stack([np.cos(twist), np.sin(twist)]).astype(np.float32),
@@ -63,35 +62,33 @@
     return (channel == wanted).astype(jnp.float32).astype(jnp.bfloat16)
 
 
-def whirl(both, middle, twist_first, twist):
-    if twist_first:
-        both = twisted(both, twist)
-    terms = dot(both, middle)
-    real, imag = (terms[:WIDTH], terms[WIDTH:])
-    both = jnp.concatenate(
-        [real[:, :WIDTH] + imag[:, WIDTH:], imag[:, :WIDTH] - real[:, WIDTH:]], 0
-    )
-    return both if twist_first else twisted(both, twist)
-
-
-def twisted(both, twist):
+def twisted(real, imag, twist):
     shape = (BLOCKS, MINE, WIDTH)
     cos, sin = (twist[0][:, None, :], twist[1][:, None, :])
-    real, imag = (both[:WIDTH].reshape(shape), both[WIDTH:].reshape(shape))
-    both = jnp.concatenate([real * cos + imag * sin, imag * cos - real * sin], 0)
-    return both.reshape(2 * WIDTH, WIDTH)
-
-
-def forward(rows, first, middle, twist):
-    return whirl(dot(first, rows), middle, True, twist)
-
-
-def inverse(real, imag, middle, last, twist):
-    return dot(last, whirl(jnp.concatenate([real, imag], 0), middle, False, twist))
+    real, imag = (real.reshape(shape), imag.reshape(shape))
+    both = [real * cos + imag * sin, imag * cos - real * sin]
+    return [part.reshape(WIDTH, WIDTH) for part in both]
+
+
+def cut(array, step, axis):
+    return [lax.slice_in_dim(array, at, at + step, axis=axis) for at in range(0, array.shape[axis], step)]
+
+
+def forward(signals, first, middle, twist):
+    both = [cut(part, WIDTH, 0) for part in cut(dot(first, jnp.concatenate(signals, 1)), WIDTH, 1)]
+    both = [jnp.concatenate(twisted(*parts, twist), 1) for parts in both]
+    return cut(dot(jnp.concatenate(both, 0), middle), WIDTH, 0)
+
+
+def inverse(spectra, middle, last, twist):
+    both = jnp.concatenate([jnp.concatenate(parts, 1) for parts in spectra], 0)
+    both = [cut(part, WIDTH, 1) for part in cut(dot(both, middle), WIDTH, 0)]
+    both = [jnp.concatenate(twisted(*parts, twist), 0) for parts in both]
+    return cut(dot(last, jnp.concatenate(both, 1)), WIDTH, 1)
 
 
 def parts_of(spectrum):
-    return (spectrum[:WIDTH], spectrum[WIDTH:])
+    return (spectrum[:, :WIDTH], spectrum[:, WIDTH:])
 
 
 def pack(upper, lower, extra):
@@ -120,42 +117,28 @@
     return (cotangent.astype(jnp.float32) * gates.astype(jnp.float32)).astype(jnp.bfloat16)
 
 
-def outgoing(order, values, gates, cotangent, filters):
-    gated = product_of(cotangent, gates)
-    across = ((1,), (1,))
-    twice = jnp.concatenate([filters, filters], 0).astype(jnp.float32)
-    return pack(dot(order, values, across), dot(order, gated, across), twice)
+def packed_rows(order, signal):
+    return dot(order, signal, ((1,), (1,)))
 
 
 def spectra(block, first, middle, last_by_channel, twist):
-    value = forward(rows_of(block, 0), first, middle, twist)
-    gated = forward(rows_of(block, 1), first, middle, twist)
+    value, gated = forward([rows_of(block, 0), rows_of(block, 1)], first, middle, twist)
     (value_r, value_i), (gated_r, gated_i) = (parts_of(value), parts_of(gated))
-    lagged = inverse(
-        gated_r * value_r + gated_i * value_i,
-        gated_r * value_i - gated_i * value_r,
-        middle, last_by_channel, twist,
-    ) * (1.0 / LENGTH)
-    lagged = lagged.reshape(MINE, BLOCKS, WIDTH)
+    lag_spec = (gated_r * value_r + gated_i * value_i, gated_r * value_i - gated_i * value_r)
+    (lagged,) = inverse([lag_spec], middle, last_by_channel, twist)
+    lagged = (lagged * (1.0 / LENGTH)).reshape(MINE, BLOCKS, WIDTH)
     return (value, gated, lagged.astype(jnp.bfloat16), extra_of(block).astype(jnp.bfloat16))
 
 
 def results(filters, total, value, gated, first_by_channel, middle, last, twist):
-    filt = forward(filters.reshape(MINE * BLOCKS, WIDTH), first_by_channel, middle, twist)
+    (filt,) = forward([filters.reshape(MINE * BLOCKS, WIDTH)], first_by_channel, middle, twist)
     (filt_r, filt_i) = parts_of(filt)
     (value_r, value_i), (gated_r, gated_i) = (parts_of(value), parts_of(gated))
+    conv_spec = (filt_r * value_r - filt_i * value_i, -filt_r * value_i - filt_i * value_r)
+    back_spec = (filt_r * gated_r + filt_i * gated_i, filt_i * gated_r - filt_r * gated_i)
+    conv, back = inverse([conv_spec, back_spec], middle, last, twist)
     scale = FACTOR / LENGTH
-    conv = inverse(
-        filt_r * value_r - filt_i * value_i,
-        -filt_r * value_i - filt_i * value_r,
-        middle, last, twist,
-    ) * scale
-    back = inverse(
-        filt_r * gated_r + filt_i * gated_i,
-        filt_i * gated_r - filt_r * gated_i,
-        middle, last, twist,
-    ) * scale
-    return pack(conv, back, total * FACTOR)
+    return pack(conv * scale, back * scale, total * FACTOR)
 
 
 def finished(place, block, values, gates, cotangent, skip_rows):
@@ -171,20 +154,23 @@
     return tuple(out.astype(jnp.bfloat16) for out in (grad_gates, grad_values, grad_filters))
 
 
-def outgoing_kernel(mp_place, values, gates, cotangent, filters, out, *scratch):
+def outgoing_kernel(place, values, gates, cotangent, filters, out, *scratch):
     held, sems = (scratch[:-1], scratch[-1])
     copies = []
     for at, (source, target) in enumerate(zip((values, gates, cotangent, filters), held)):
         copies.append(pltpu.make_async_copy(source, target, sems.at[at]))
         copies[-1].start()
-    order = order_of(mp_place[0])
+    order = order_of(place[0] & 15)
     for copy in copies:
         copy.wait()
-    out[...] = outgoing(order, *(ref[...] for ref in held))
-
-
-def spectra_kernel(ctx_half, mp_place, *refs):
-    half, place = (ctx_half[0], mp_place[0])
+    value_rows = packed_rows(order, held[0][...])
+    gated_rows = packed_rows(order, product_of(held[2][...], held[1][...]))
+    filter_rows = jnp.concatenate([held[3][...]] * 2, 0).astype(jnp.float32)
+    out[...] = pack(value_rows, gated_rows, filter_rows)
+
+
+def spectra_kernel(place, *refs):
+    half, place = (place[0] >> 4, place[0] & 15)
     value, gated, own, sent = refs[-4:]
     value[...], gated[...], lagged, own_rows = spectra(*(ref[...] for ref in refs[:-4]))
     own[...] = own_rows
@@ -193,8 +179,8 @@
         sent[source_of(half, row, place)] = lagged[row]
 
 
-def results_kernel(ctx_half, mp_place, arrived, own, *refs):
-    half, place = (ctx_half[0], mp_place[0])
+def results_kernel(place, arrived, own, *refs):
+    half, place = (place[0] >> 4, place[0] & 15)
     held = source_of(half, 0, place) == place
     filters = [jnp.where(held, own[...], arrived[source_of(half, 0, place)])]
     filters += [arrived[source_of(half, row, place)] for row in range(1, MINE)]
@@ -206,8 +192,8 @@
     refs[-1][...] = results(jnp.stack(filters), total, *(ref[...] for ref in refs[:-1]))
 
 
-def finished_kernel(mp_place, *refs):
-    outs = finished(mp_place[0], *(ref[...] for ref in refs[:-3]))
+def finished_kernel(place, *refs):
+    outs = finished(place[0] & 15, *(ref[...] for ref in refs[:-3]))
     for ref, out in zip(refs[-3:], outs):
         ref[...] = out
 
@@ -220,6 +206,7 @@
     single = len(outs) == 1
     scratch = []
     if fetched:
+        args = (*args[:scalars], *(pltpu.with_memory_space_constraint(arg, pltpu.HBM) for arg in args[scalars:]))
         scratch = [pltpu.VMEM(arg.shape, arg.dtype) for arg in args[scalars:]]
         scratch.append(pltpu.SemaphoreType.DMA((len(scratch),)))
     return pl.pallas_call(
@@ -228,7 +215,7 @@
         in_specs=[scalar] * scalars + [given] * (len(args) - scalars),
         out_specs=whole if single else (whole,) * len(outs),
         scratch_shapes=scratch,
-        compiler_params=pltpu.CompilerParams(vmem_limit_bytes=MOST if fetched else VMEM),
+        compiler_params=pltpu.CompilerParams(vmem_limit_bytes=VMEM),
         cost_estimate=pl.CostEstimate(flops=flops, bytes_accessed=size, transcendentals=0),
     )(*args)
 
@@ -239,34 +226,33 @@
 
 def per_device(table, values, gates, cotangent, filters, skip_gain):
     shape = functools.partial(jax.ShapeDtypeStruct, dtype=jnp.bfloat16)
-    spectrum = jax.ShapeDtypeStruct((2 * WIDTH, WIDTH), jnp.float32)
+    spectrum = jax.ShapeDtypeStruct((WIDTH, 2 * WIDTH), jnp.float32)
     packed = shape((BLOCKS, 2, 8 * WIDTH + 128))
-    ctx_half = (lax.axis_index("ctx") // HALF).astype(jnp.int32).reshape(1)
-    mp_place = lax.axis_index("mp").astype(jnp.int32).reshape(1)
+    place = (lax.axis_index("ctx") // HALF * SHARDS + lax.axis_index("mp")).astype(jnp.int32).reshape(1)
     skip_rows = jnp.broadcast_to(skip_gain[None, :], (8, WIDTH))
     cube = 2 * WIDTH**3
 
     block = call(
-        outgoing_kernel, (packed,), (mp_place, values, gates, cotangent, filters.T),
+        outgoing_kernel, (packed,), (place, values, gates, cotangent, filters.T),
         2 * cube, scalars=1, fetched=True,
     )
     block = swap(block, "ctx")
     value, gated, own, sent = call(
         spectra_kernel,
         (spectrum, spectrum, shape((BLOCKS, WIDTH)), shape((SHARDS, BLOCKS, WIDTH))),
-        (ctx_half, mp_place, block, table["first"], table["middle"], table["last_by_channel"], table["twist"]),
-        18 * cube, scalars=2,
+        (place, block, table["first"], table["middle"], table["last_by_channel"], table["twist"]),
+        18 * cube, scalars=1,
     )
     sent = swap(sent, "mp")
     block = call(
         results_kernel, (packed,),
-        (ctx_half, mp_place, sent, own, value, gated, table["first_by_channel"], table["middle"], table["last"], table["twist"]),
-        18 * cube, scalars=2,
+        (place, sent, own, value, gated, table["first_by_channel"], table["middle"], table["last"], table["twist"]),
+        18 * cube, scalars=1,
     )
     block = swap(block, "ctx")
     grad_gates, grad_values, grad_filters = call(
         finished_kernel, (shape(values.shape), shape(values.shape), shape((HALF, WIDTH))),
-        (mp_place, block, values, gates, cotangent, skip_rows), 2 * cube, scalars=1,
+        (place, block, values, gates, cotangent, skip_rows), 2 * cube, scalars=1,
     )
     return (grad_gates, grad_values, grad_filters.T)
 

time: 87.6 us -> 86.2 us (0.984)
  blocking collectives: 41.5 us -> 78.9 us
  waiting for transfers between devices: 20.5 us -> 0 us
  starting transfers between devices: 17.1 us -> 0 us
  Pallas kernels: 6.16 us -> 4.98 us
    all_to_all x2 -> x3, blocking collectives: 41.5 us -> 78.9 us  [swap(): return lax.all_to_all(block, axis, split_axis=0, concat_axis=0, tiled=True)]
    all_to_all x1 -> x0, waiting for transfers between devices: 20.5 us -> none  [swap(): return lax.all_to_all(block, axis, split_axis=0, concat_axis=0, tiled=True)]
    all_to_all x1 -> x0, starting transfers between devices: 17.1 us -> none  [swap(): return lax.all_to_all(block, axis, split_axis=0, concat_axis=0, tiled=True)]
    pallas_call x4, Pallas kernels: 6.16 us -> 4.98 us  [call(): pl.pallas_call(kernel, out_shape=outs[0] if single else outs, in_specs=[s...]
  transfers between devices with their start and end apart: 1 -> 0, of which waited for: 1 -> 0; matrix products, arithmetic and copies ran while one was open for 0% -> 0% of each run, Pallas kernels for 0% -> 0%
where the time goes in v5:
time: 86.2 us; the launch traced here: 84.7 us
  blocking collectives  78.9 us (92%)
  Pallas kernels  4.98 us (6%)
    all_to_all x3, blocking collectives, swap(): return lax.all_to_all(block, axis, split_axis=0, concat_axis=0, tiled=True)  78.9 us
    pallas_call x4, Pallas kernels, call(): pl.pallas_call(kernel, out_shape=outs[0] if single else outs, in_specs=[s...  4.98 us

profile of v5, /device:TPU:1, one launch (start us, length us, event | category | flops | bytes accessed | tf_op | source)
XLA Modules:
  0.0 84.7 jit_solution(16181006013921889480)
XLA Ops:
  0.6 0.0 copy-start
  0.7 0.0 copy-start.8
  0.7 1.5 %shard_map.130 = bf16[32,2,2176]{2,1,0:T(2,128)(2,1)S(1)} custom-call(s32[1]{0:T(128)} %bitcast.place, bf16[256,256]{1,0:T(8,128)(2,1)} %refs_1_.2, bf16[256,256]{1,0:T(8,128)(2,1)} %refs_2_.3, bf16[256,256]{1,0:T(8,128)(2,1)} %refs_3_.3, bf16[16,256]{1,0:T(8,128)(2,1)} %bitcast.3), custom_call_target="tpu_custom_call" | custom-call | flops 67108864 | bytes 679940 | tf_op jit(solution)/shard_map/pallas_call | solution.py:212
  2.2 0.0 copy-start.6
  2.2 0.0 copy-start.7
  2.2 37.4 %all_to_all.15.refs_0_ = bf16[32,2,2176]{2,1,0:T(2,128)(2,1)S(1)} all-to-all(bf16[32,2,2176]{2,1,0:T(2,128)(2,1)S(1)} %shard_map.130), channel_id=1, replica_groups=mesh['ctx'=32,'mp'=16] {'ctx'}, dimensions={0} | all-to-all | bytes 557056 | tf_op jit(solution)/shard_map/all_to_all | solution.py:224
  39.6 0.0 copy-done
  39.6 0.0 copy-done.8
  39.6 0.0 copy-done.6
  39.6 0.0 copy-done.7
  39.6 1.2 %shard_map.131 = (f32[256,512]{1,0:T(8,128)S(1)}, f32[256,512]{1,0:T(8,128)S(1)}, bf16[32,256]{1,0:T(8,128)(2,1)S(1)}, bf16[16,32,256]{2,1,0:T(8,128)(2,1)S(1)}) custom-call(s32[1]{0:T(128)} %bitcast.place, bf16[32,2,2176]{2,1,0:T(2,128)(2,1)S(1)} %all_to_all.15.refs_0_, bf16[512,256]{1,0:T(8,128)(2,1)S(1)} %copy-done.7, bf16[512,512]{1,0:T(8,128)(2,1)S(1)} %copy-done, ...), custom_call_target="tpu_custom_call" | custom-call | flops 603979776 | bytes 2719748 | tf_op jit(solution)/shard_map/pallas_call | solution.py:212
  40.8 0.0 copy-start.4
  40.8 0.0 copy-start.5
  40.8 18.2 %all_to_all.16.arrived = bf16[16,32,256]{2,1,0:T(8,128)(2,1)S(1)} all-to-all(bf16[16,32,256]{2,1,0:T(8,128)(2,1)S(1)} %get-tuple-element.10), channel_id=1, replica_groups=mesh['ctx'=32,'mp'=16] {'mp'}, dimensions={0} | all-to-all | bytes 524288 | tf_op jit(solution)/shard_map/all_to_all | solution.py:224
  59.0 0.0 copy-done.5
  59.0 1.2 %shard_map.132 = bf16[32,2,2176]{2,1,0:T(2,128)(2,1)S(1)} custom-call(s32[1]{0:T(128)} %bitcast.place, bf16[16,32,256]{2,1,0:T(8,128)(2,1)S(1)} %all_to_all.16.arrived, bf16[32,256]{1,0:T(8,128)(2,1)S(1)} %get-tuple-element.11.own, f32[256,512]{1,0:T(8,128)S(1)} %get-tuple-element.12.refs_0_, f32[256,512]{1,0:T(8,128)S(1)} %get-tuple-element.13.refs_1_, ...), custom_call_target="tpu_custom_call" | custom-call | flops 603979776 | bytes 2719748 | tf_op jit(solution)/shard_map/pallas_call | solution.py:212
  60.2 0.0 copy-start.9
  60.3 0.0 copy-start.1
  60.3 0.0 copy-start.2
  60.3 0.0 copy-start.3
  60.3 23.3 %all_to_all.17.refs_0_ = bf16[32,2,2176]{2,1,0:T(2,128)(2,1)S(1)} all-to-all(bf16[32,2,2176]{2,1,0:T(2,128)(2,1)S(1)} %shard_map.132), channel_id=1, replica_groups=mesh['ctx'=32,'mp'=16] {'ctx'}, dimensions={0} | all-to-all | bytes 557056 | tf_op jit(solution)/shard_map/all_to_all | solution.py:224
  83.6 0.0 copy-done.1
  83.6 0.0 copy-done.3
  83.6 1.1 %shard_map.133 = (bf16[256,256]{1,0:T(8,128)(2,1)}, bf16[256,256]{1,0:T(8,128)(2,1)}, bf16[16,256]{1,0:T(8,128)(2,1)}) custom-call(s32[1]{0:T(128)} %bitcast.place, bf16[32,2,2176]{2,1,0:T(2,128)(2,1)S(1)} %all_to_all.17.refs_0_, bf16[256,256]{1,0:T(8,128)(2,1)S(1)} %copy-done.1, bf16[256,256]{1,0:T(8,128)(2,1)S(1)} %copy-done.2, ...), custom_call_target="tpu_custom_call" | custom-call | flops 67108864 | bytes 950276 | tf_op jit(solution)/shard_map/pallas_call | solution.py:212
  (4 shorter events, 0.0 us)
Async XLA Ops:
  0.6 39.0 %copy-start = (bf16[512,512]{1,0:T(8,128)(2,1)S(1)}, bf16[512,512]{1,0:T(8,128)(2,1)}, u32[]{:S(2)}) copy-start(bf16[512,512]{1,0:T(8,128)(2,1)} %constant.39.clone.refs_2_.refs_3_) | copy-start | bytes 1572868
  0.7 38.9 %copy-start.8 = (bf16[256,512]{1,0:T(8,128)(2,1)S(1)}, bf16[256,512]{1,0:T(8,128)(2,1)}, u32[]{:S(2)}) copy-start(bf16[256,512]{1,0:T(8,128)(2,1)} %constant.40.clone.refs_3_) | copy-start | bytes 786436
  2.2 37.4 %copy-start.6 = (f32[2,32,256]{2,1,0:T(8,128)S(1)}, f32[2,32,256]{2,1,0:T(8,128)}, u32[]{:S(2)}) copy-start(f32[2,32,256]{2,1,0:T(8,128)} %constant.41.clone.refs_4_.refs_5_) | copy-start | bytes 196612
  2.2 37.4 %copy-start.7 = (bf16[512,256]{1,0:T(8,128)(2,1)S(1)}, bf16[512,256]{1,0:T(8,128)(2,1)}, u32[]{:S(2)}) copy-start(bf16[512,256]{1,0:T(8,128)(2,1)} %constant.38.clone.refs_1_) | copy-start | bytes 786436
  40.8 18.2 %copy-start.4 = (bf16[512,256]{1,0:T(8,128)(2,1)S(1)}, bf16[512,256]{1,0:T(8,128)(2,1)}, u32[]{:S(2)}) copy-start(bf16[512,256]{1,0:T(8,128)(2,1)} %constant.42.clone.refs_2_) | copy-start | bytes 786436
  40.8 18.2 %copy-start.5 = (bf16[256,512]{1,0:T(8,128)(2,1)S(1)}, bf16[256,512]{1,0:T(8,128)(2,1)}, u32[]{:S(2)}) copy-start(bf16[256,512]{1,0:T(8,128)(2,1)} %constant.43.clone.refs_4_) | copy-start | bytes 786436
  60.2 23.4 %copy-start.9 = (f32[256]{0:T(256)S(1)}, f32[256]{0:T(256)}, u32[]{:S(2)}) copy-start(f32[256]{0:T(256)} %param.15) | copy-start | bytes 3076
  60.3 23.4 %copy-start.1 = (bf16[256,256]{1,0:T(8,128)(2,1)S(1)}, bf16[256,256]{1,0:T(8,128)(2,1)}, u32[]{:S(2)}) copy-start(bf16[256,256]{1,0:T(8,128)(2,1)} %refs_1_.2) | copy-start | bytes 393220
  60.3 23.4 %copy-start.2 = (bf16[256,256]{1,0:T(8,128)(2,1)S(1)}, bf16[256,256]{1,0:T(8,128)(2,1)}, u32[]{:S(2)}) copy-start(bf16[256,256]{1,0:T(8,128)(2,1)} %refs_2_.3) | copy-start | bytes 393220
  60.3 23.4 %copy-start.3 = (bf16[256,256]{1,0:T(8,128)(2,1)S(1)}, bf16[256,256]{1,0:T(8,128)(2,1)}, u32[]{:S(2)}) copy-start(bf16[256,256]{1,0:T(8,128)(2,1)} %refs_3_.3) | copy-start | bytes 393220

commit v6 on v5

--- a/solution.py
+++ b/solution.py
@@ -15,13 +15,15 @@
 WIDTH = 256
 LENGTH = BLOCKS * WIDTH
 SHARDS = 16
+ORDER = tuple(HALF * x + z for z in (8, 9, 10, 15, 11, 14, 12, 7, 6, 13, 4, 5, 3, 2, 1, 0) for x in (0, 1))
+LATER = sum(1 << device for device in ORDER[HALF:])
 FACTOR = 1.0 / math.sqrt(LENGTH)
 VMEM = 32 * 1024 * 1024
 
 
 def tables():
     quarter = np.arange(BLOCKS) + 0.25
-    outer = 2.0 * np.pi * np.outer(quarter, np.arange(BLOCKS)) / BLOCKS
+    outer = 2.0 * np.pi * np.outer(quarter, ORDER) / BLOCKS
     eye = np.eye(MINE)
     cos_rows = np.kron(np.cos(outer), eye)
     sin_rows = np.kron(np.sin(outer), eye)
@@ -220,15 +222,16 @@
     )(*args)
 
 
-def swap(block, axis):
-    return lax.all_to_all(block, axis, split_axis=0, concat_axis=0, tiled=True)
+def swap(block, axis, groups=None):
+    return lax.all_to_all(block, axis, split_axis=0, concat_axis=0, tiled=True, axis_index_groups=groups)
 
 
 def per_device(table, values, gates, cotangent, filters, skip_gain):
     shape = functools.partial(jax.ShapeDtypeStruct, dtype=jnp.bfloat16)
     spectrum = jax.ShapeDtypeStruct((WIDTH, 2 * WIDTH), jnp.float32)
     packed = shape((BLOCKS, 2, 8 * WIDTH + 128))
-    place = (lax.axis_index("ctx") // HALF * SHARDS + lax.axis_index("mp")).astype(jnp.int32).reshape(1)
+    later = lax.shift_right_logical(np.uint32(LATER), lax.axis_index("ctx").astype(jnp.uint32)) & 1
+    place = (later.astype(jnp.int32) * SHARDS + lax.axis_index("mp")).reshape(1)
     skip_rows = jnp.broadcast_to(skip_gain[None, :], (8, WIDTH))
     cube = 2 * WIDTH**3
 
@@ -236,7 +239,7 @@
         outgoing_kernel, (packed,), (place, values, gates, cotangent, filters.T),
         2 * cube, scalars=1, fetched=True,
     )
-    block = swap(block, "ctx")
+    block = swap(block, "ctx", [ORDER])
     value, gated, own, sent = call(
         spectra_kernel,
         (spectrum, spectrum, shape((BLOCKS, WIDTH)), shape((SHARDS, BLOCKS, WIDTH))),
@@ -249,7 +252,7 @@
         (place, sent, own, value, gated, table["first_by_channel"], table["middle"], table["last"], table["twist"]),
         18 * cube, scalars=1,
     )
-    block = swap(block, "ctx")
+    block = swap(block, "ctx", [ORDER])
     grad_gates, grad_values, grad_filters = call(
         finished_kernel, (shape(values.shape), shape(values.shape), shape((HALF, WIDTH))),
         (place, block, values, gates, cotangent, skip_rows), 2 * cube, scalars=1,

time: 86.2 us -> 80.2 us (0.930); the launches traced: 84.7 us -> 80 us
  blocking collectives: 78.9 us -> 74.2 us
    all_to_all x3, blocking collectives: 78.9 us -> 74.2 us  [swap(): lax.all_to_all(block, axis, split_axis=0, concat_axis=0, tiled=True, axis...]
where the time goes in v6:
time: 80.2 us; the launch traced here: 80 us
  blocking collectives  74.2 us (93%)
  Pallas kernels  4.98 us (6%)
    all_to_all x3, blocking collectives, swap(): lax.all_to_all(block, axis, split_axis=0, concat_axis=0, tiled=True, axis...  74.2 us
    pallas_call x4, Pallas kernels, call(): pl.pallas_call(kernel, out_shape=outs[0] if single else outs, in_specs=[s...  4.98 us

profile of v6, /device:TPU:1, one launch (start us, length us, event | category | flops | bytes accessed | tf_op | source)
XLA Modules:
  0.0 80.0 jit_solution(15036081905653085076)
XLA Ops:
  0.6 0.0 copy-start
  0.7 0.0 copy-start.8
  0.7 1.5 %shard_map.130 = bf16[32,2,2176]{2,1,0:T(2,128)(2,1)S(1)} custom-call(s32[1]{0:T(128)} %bitcast.place, bf16[256,256]{1,0:T(8,128)(2,1)} %refs_1_.2, bf16[256,256]{1,0:T(8,128)(2,1)} %refs_2_.3, bf16[256,256]{1,0:T(8,128)(2,1)} %refs_3_.3, bf16[16,256]{1,0:T(8,128)(2,1)} %bitcast.3), custom_call_target="tpu_custom_call" | custom-call | flops 67108864 | bytes 679940 | tf_op jit(solution)/shard_map/pallas_call | solution.py:214
  2.2 0.0 copy-start.6
  2.2 0.0 copy-start.7
  2.2 32.6 %all_to_all.15.refs_0_ = bf16[32,2,2176]{2,1,0:T(2,128)(2,1)S(1)} all-to-all(bf16[32,2,2176]{2,1,0:T(2,128)(2,1)S(1)} %shard_map.130), channel_id=1, replica_groups={{128,384,144,400,160,416,240,496,176,432,224,480,192,448,112,368,96,352..., dimensions={0} | all-to-all | bytes 557056 | tf_op jit(solution)/shard_map/all_to_all | solution.py:226
  34.8 0.0 copy-done
  34.8 0.0 copy-done.8
  34.8 0.0 copy-done.6
  34.8 0.0 copy-done.7
  34.9 1.2 %shard_map.131 = (f32[256,512]{1,0:T(8,128)S(1)}, f32[256,512]{1,0:T(8,128)S(1)}, bf16[32,256]{1,0:T(8,128)(2,1)S(1)}, bf16[16,32,256]{2,1,0:T(8,128)(2,1)S(1)}) custom-call(s32[1]{0:T(128)} %bitcast.place, bf16[32,2,2176]{2,1,0:T(2,128)(2,1)S(1)} %all_to_all.15.refs_0_, bf16[512,256]{1,0:T(8,128)(2,1)S(1)} %copy-done.7, bf16[512,512]{1,0:T(8,128)(2,1)S(1)} %copy-done, ...), custom_call_target="tpu_custom_call" | custom-call | flops 603979776 | bytes 2719748 | tf_op jit(solution)/shard_map/pallas_call | solution.py:214
  36.0 0.0 copy-start.4
  36.0 0.0 copy-start.5
  36.0 17.0 %all_to_all.16.arrived = bf16[16,32,256]{2,1,0:T(8,128)(2,1)S(1)} all-to-all(bf16[16,32,256]{2,1,0:T(8,128)(2,1)S(1)} %get-tuple-element.10), channel_id=1, replica_groups=mesh['ctx'=32,'mp'=16] {'mp'}, dimensions={0} | all-to-all | bytes 524288 | tf_op jit(solution)/shard_map/all_to_all | solution.py:226
  53.1 0.0 copy-done.5
  53.1 1.2 %shard_map.132 = bf16[32,2,2176]{2,1,0:T(2,128)(2,1)S(1)} custom-call(s32[1]{0:T(128)} %bitcast.place, bf16[16,32,256]{2,1,0:T(8,128)(2,1)S(1)} %all_to_all.16.arrived, bf16[32,256]{1,0:T(8,128)(2,1)S(1)} %get-tuple-element.11.own, f32[256,512]{1,0:T(8,128)S(1)} %get-tuple-element.12.refs_0_, f32[256,512]{1,0:T(8,128)S(1)} %get-tuple-element.13.refs_1_, ...), custom_call_target="tpu_custom_call" | custom-call | flops 603979776 | bytes 2719748 | tf_op jit(solution)/shard_map/pallas_call | solution.py:214
  54.3 0.0 copy-start.9
  54.4 0.0 copy-start.1
  54.4 0.0 copy-start.2
  54.4 0.0 copy-start.3
  54.4 24.5 %all_to_all.17.refs_0_ = bf16[32,2,2176]{2,1,0:T(2,128)(2,1)S(1)} all-to-all(bf16[32,2,2176]{2,1,0:T(2,128)(2,1)S(1)} %shard_map.132), channel_id=1, replica_groups={{128,384,144,400,160,416,240,496,176,432,224,480,192,448,112,368,96,352..., dimensions={0} | all-to-all | bytes 557056 | tf_op jit(solution)/shard_map/all_to_all | solution.py:226
  78.9 0.0 copy-done.9
  78.9 0.0 copy-done.3
  78.9 1.1 %shard_map.133 = (bf16[256,256]{1,0:T(8,128)(2,1)}, bf16[256,256]{1,0:T(8,128)(2,1)}, bf16[16,256]{1,0:T(8,128)(2,1)}) custom-call(s32[1]{0:T(128)} %bitcast.place, bf16[32,2,2176]{2,1,0:T(2,128)(2,1)S(1)} %all_to_all.17.refs_0_, bf16[256,256]{1,0:T(8,128)(2,1)S(1)} %copy-done.1, bf16[256,256]{1,0:T(8,128)(2,1)S(1)} %copy-done.2, ...), custom_call_target="tpu_custom_call" | custom-call | flops 67108864 | bytes 950276 | tf_op jit(solution)/shard_map/pallas_call | solution.py:214
  (4 shorter events, 0.0 us)
Async XLA Ops:
  0.6 34.2 %copy-start = (bf16[512,512]{1,0:T(8,128)(2,1)S(1)}, bf16[512,512]{1,0:T(8,128)(2,1)}, u32[]{:S(2)}) copy-start(bf16[512,512]{1,0:T(8,128)(2,1)} %constant.27.clone.refs_2_.refs_3_) | copy-start | bytes 1572868
  0.7 34.2 %copy-start.8 = (bf16[256,512]{1,0:T(8,128)(2,1)S(1)}, bf16[256,512]{1,0:T(8,128)(2,1)}, u32[]{:S(2)}) copy-start(bf16[256,512]{1,0:T(8,128)(2,1)} %constant.28.clone.refs_3_) | copy-start | bytes 786436
  2.2 32.7 %copy-start.6 = (f32[2,32,256]{2,1,0:T(8,128)S(1)}, f32[2,32,256]{2,1,0:T(8,128)}, u32[]{:S(2)}) copy-start(f32[2,32,256]{2,1,0:T(8,128)} %constant.29.clone.refs_4_.refs_5_) | copy-start | bytes 196612
  2.2 32.7 %copy-start.7 = (bf16[512,256]{1,0:T(8,128)(2,1)S(1)}, bf16[512,256]{1,0:T(8,128)(2,1)}, u32[]{:S(2)}) copy-start(bf16[512,256]{1,0:T(8,128)(2,1)} %constant.26.clone.refs_1_) | copy-start | bytes 786436
  36.0 17.1 %copy-start.4 = (bf16[512,256]{1,0:T(8,128)(2,1)S(1)}, bf16[512,256]{1,0:T(8,128)(2,1)}, u32[]{:S(2)}) copy-start(bf16[512,256]{1,0:T(8,128)(2,1)} %constant.30.clone.refs_2_) | copy-start | bytes 786436
  36.0 17.1 %copy-start.5 = (bf16[256,512]{1,0:T(8,128)(2,1)S(1)}, bf16[256,512]{1,0:T(8,128)(2,1)}, u32[]{:S(2)}) copy-start(bf16[256,512]{1,0:T(8,128)(2,1)} %constant.31.clone.refs_4_) | copy-start | bytes 786436
  54.3 24.6 %copy-start.9 = (f32[256]{0:T(256)S(1)}, f32[256]{0:T(256)}, u32[]{:S(2)}) copy-start(f32[256]{0:T(256)} %param.15) | copy-start | bytes 3076
  54.4 24.6 %copy-start.1 = (bf16[256,256]{1,0:T(8,128)(2,1)S(1)}, bf16[256,256]{1,0:T(8,128)(2,1)}, u32[]{:S(2)}) copy-start(bf16[256,256]{1,0:T(8,128)(2,1)} %refs_1_.2) | copy-start | bytes 393220
  54.4 24.5 %copy-start.2 = (bf16[256,256]{1,0:T(8,128)(2,1)S(1)}, bf16[256,256]{1,0:T(8,128)(2,1)}, u32[]{:S(2)}) copy-start(bf16[256,256]{1,0:T(8,128)(2,1)} %refs_2_.3) | copy-start | bytes 393220
  54.4 24.5 %copy-start.3 = (bf16[256,256]{1,0:T(8,128)(2,1)S(1)}, bf16[256,256]{1,0:T(8,128)(2,1)}, u32[]{:S(2)}) copy-start(bf16[256,256]{1,0:T(8,128)(2,1)} %refs_3_.3) | copy-start | bytes 393220

commit v7 on v6

--- a/solution.py
+++ b/solution.py
@@ -16,6 +16,7 @@
 LENGTH = BLOCKS * WIDTH
 SHARDS = 16
 ORDER = tuple(HALF * x + z for z in (8, 9, 10, 15, 11, 14, 12, 7, 6, 13, 4, 5, 3, 2, 1, 0) for x in (0, 1))
+MP_ORDER = tuple(range(SHARDS))[::-1]
 LATER = sum(1 << device for device in ORDER[HALF:])
 FACTOR = 1.0 / math.sqrt(LENGTH)
 VMEM = 32 * 1024 * 1024
@@ -53,14 +54,18 @@
     )
 
 
+def shard_at(place):
+    return SHARDS - 1 - place
+
+
 def source_of(half, row, place):
     return jnp.where(row == 0, 8 * half + (place & 7), (place - row - 8 * half) & 15)
 
 
 def order_of(place):
-    row = lax.broadcasted_iota(jnp.int32, (WIDTH, WIDTH), 0)
+    row = lax.broadcasted_iota(jnp.int32, (WIDTH, 1), 0)
     channel = lax.broadcasted_iota(jnp.int32, (WIDTH, WIDTH), 1)
-    wanted = 16 * source_of(row >> 7, row & 7, place) + ((row >> 3) & 15)
+    wanted = 16 * shard_at(source_of(row >> 7, row & 7, place)) + ((row >> 3) & 15)
     return (channel == wanted).astype(jnp.float32).astype(jnp.bfloat16)
 
 
@@ -231,7 +236,7 @@
     spectrum = jax.ShapeDtypeStruct((WIDTH, 2 * WIDTH), jnp.float32)
     packed = shape((BLOCKS, 2, 8 * WIDTH + 128))
     later = lax.shift_right_logical(np.uint32(LATER), lax.axis_index("ctx").astype(jnp.uint32)) & 1
-    place = (later.astype(jnp.int32) * SHARDS + lax.axis_index("mp")).reshape(1)
+    place = (later.astype(jnp.int32) * SHARDS + shard_at(lax.axis_index("mp"))).reshape(1)
     skip_rows = jnp.broadcast_to(skip_gain[None, :], (8, WIDTH))
     cube = 2 * WIDTH**3
 
@@ -246,7 +251,7 @@
         (place, block, table["first"], table["middle"], table["last_by_channel"], table["twist"]),
         18 * cube, scalars=1,
     )
-    sent = swap(sent, "mp")
+    sent = swap(sent, "mp", [MP_ORDER])
     block = call(
         results_kernel, (packed,),
         (place, sent, own, value, gated, table["first_by_channel"], table["middle"], table["last"], table["twist"]),

time: 80.2 us -> 78 us (0.973)
  blocking collectives: 74.2 us -> 71.9 us
    all_to_all x3, blocking collectives: 74.2 us -> 71.9 us  [swap(): lax.all_to_all(block, axis, split_axis=0, concat_axis=0, tiled=True, axis...]
where the time goes in v7:
time: 78 us; the launch traced here: 77.7 us
  blocking collectives  71.9 us (92%)
  Pallas kernels  4.99 us (6%)
    all_to_all x3, blocking collectives, swap(): lax.all_to_all(block, axis, split_axis=0, concat_axis=0, tiled=True, axis...  71.9 us
    pallas_call x4, Pallas kernels, call(): pl.pallas_call(kernel, out_shape=outs[0] if single else outs, in_specs=[s...  4.99 us

profile of v7, /device:TPU:1, one launch (start us, length us, event | category | flops | bytes accessed | tf_op | source)
XLA Modules:
  0.0 77.7 jit_solution(2728868036202869865)
XLA Ops:
  0.6 0.0 copy-start
  0.7 0.0 copy-start.8
  0.7 1.5 %shard_map.130 = bf16[32,2,2176]{2,1,0:T(2,128)(2,1)S(1)} custom-call(s32[1]{0:T(128)} %bitcast.place, bf16[256,256]{1,0:T(8,128)(2,1)} %refs_1_.2, bf16[256,256]{1,0:T(8,128)(2,1)} %refs_2_.3, bf16[256,256]{1,0:T(8,128)(2,1)} %refs_3_.3, bf16[16,256]{1,0:T(8,128)(2,1)} %bitcast.3), custom_call_target="tpu_custom_call" | custom-call | flops 67108864 | bytes 679940 | tf_op jit(solution)/shard_map/pallas_call | solution.py:219
  2.2 0.0 copy-start.6
  2.2 0.0 copy-start.7
  2.2 32.6 %all_to_all.15.refs_0_ = bf16[32,2,2176]{2,1,0:T(2,128)(2,1)S(1)} all-to-all(bf16[32,2,2176]{2,1,0:T(2,128)(2,1)S(1)} %shard_map.130), channel_id=1, replica_groups={{128,384,144,400,160,416,240,496,176,432,224,480,192,448,112,368,96,352..., dimensions={0} | all-to-all | bytes 557056 | tf_op jit(solution)/shard_map/all_to_all | solution.py:231
  34.8 0.0 copy-done
  34.8 0.0 copy-done.8
  34.8 0.0 copy-done.6
  34.9 0.0 copy-done.7
  34.9 1.2 %shard_map.131 = (f32[256,512]{1,0:T(8,128)S(1)}, f32[256,512]{1,0:T(8,128)S(1)}, bf16[32,256]{1,0:T(8,128)(2,1)S(1)}, bf16[16,32,256]{2,1,0:T(8,128)(2,1)S(1)}) custom-call(s32[1]{0:T(128)} %bitcast.place, bf16[32,2,2176]{2,1,0:T(2,128)(2,1)S(1)} %all_to_all.15.refs_0_, bf16[512,256]{1,0:T(8,128)(2,1)S(1)} %copy-done.7, bf16[512,512]{1,0:T(8,128)(2,1)S(1)} %copy-done, ...), custom_call_target="tpu_custom_call" | custom-call | flops 603979776 | bytes 2719748 | tf_op jit(solution)/shard_map/pallas_call | solution.py:219
  36.0 0.0 copy-start.4
  36.0 0.0 copy-start.5
  36.0 13.8 %all_to_all.16.arrived = bf16[16,32,256]{2,1,0:T(8,128)(2,1)S(1)} all-to-all(bf16[16,32,256]{2,1,0:T(8,128)(2,1)S(1)} %get-tuple-element.10), channel_id=1, replica_groups={{15,14,13,12,11,10,9,8,7,6,5,4,3,2,1,0},{31,30,29,28,27,26,25,24,23,22,..., dimensions={0} | all-to-all | bytes 524288 | tf_op jit(solution)/shard_map/all_to_all | solution.py:231
  49.8 0.0 copy-done.4
  49.8 0.0 copy-done.5
  49.8 1.2 %shard_map.132 = bf16[32,2,2176]{2,1,0:T(2,128)(2,1)S(1)} custom-call(s32[1]{0:T(128)} %bitcast.place, bf16[16,32,256]{2,1,0:T(8,128)(2,1)S(1)} %all_to_all.16.arrived, bf16[32,256]{1,0:T(8,128)(2,1)S(1)} %get-tuple-element.11.own, f32[256,512]{1,0:T(8,128)S(1)} %get-tuple-element.12.refs_0_, f32[256,512]{1,0:T(8,128)S(1)} %get-tuple-element.13.refs_1_, ...), custom_call_target="tpu_custom_call" | custom-call | flops 603979776 | bytes 2719748 | tf_op jit(solution)/shard_map/pallas_call | solution.py:219
  51.1 0.0 copy-start.9
  51.1 0.0 copy-start.1
  51.1 0.0 copy-start.2
  51.1 0.0 copy-start.3
  51.1 25.5 %all_to_all.17.refs_0_ = bf16[32,2,2176]{2,1,0:T(2,128)(2,1)S(1)} all-to-all(bf16[32,2,2176]{2,1,0:T(2,128)(2,1)S(1)} %shard_map.132), channel_id=1, replica_groups={{128,384,144,400,160,416,240,496,176,432,224,480,192,448,112,368,96,352..., dimensions={0} | all-to-all | bytes 557056 | tf_op jit(solution)/shard_map/all_to_all | solution.py:231
  76.6 0.0 copy-done.9
  76.7 1.1 %shard_map.133 = (bf16[256,256]{1,0:T(8,128)(2,1)}, bf16[256,256]{1,0:T(8,128)(2,1)}, bf16[16,256]{1,0:T(8,128)(2,1)}) custom-call(s32[1]{0:T(128)} %bitcast.place, bf16[32,2,2176]{2,1,0:T(2,128)(2,1)S(1)} %all_to_all.17.refs_0_, bf16[256,256]{1,0:T(8,128)(2,1)S(1)} %copy-done.1, bf16[256,256]{1,0:T(8,128)(2,1)S(1)} %copy-done.2, ...), custom_call_target="tpu_custom_call" | custom-call | flops 67108864 | bytes 950276 | tf_op jit(solution)/shard_map/pallas_call | solution.py:219
  (4 shorter events, 0.0 us)
Async XLA Ops:
  0.6 34.2 %copy-start = (bf16[512,512]{1,0:T(8,128)(2,1)S(1)}, bf16[512,512]{1,0:T(8,128)(2,1)}, u32[]{:S(2)}) copy-start(bf16[512,512]{1,0:T(8,128)(2,1)} %constant.29.clone.refs_2_.refs_3_) | copy-start | bytes 1572868
  0.7 34.2 %copy-start.8 = (bf16[256,512]{1,0:T(8,128)(2,1)S(1)}, bf16[256,512]{1,0:T(8,128)(2,1)}, u32[]{:S(2)}) copy-start(bf16[256,512]{1,0:T(8,128)(2,1)} %constant.30.clone.refs_3_) | copy-start | bytes 786436
  2.2 32.7 %copy-start.6 = (f32[2,32,256]{2,1,0:T(8,128)S(1)}, f32[2,32,256]{2,1,0:T(8,128)}, u32[]{:S(2)}) copy-start(f32[2,32,256]{2,1,0:T(8,128)} %constant.31.clone.refs_4_.refs_5_) | copy-start | bytes 196612
  2.2 32.7 %copy-start.7 = (bf16[512,256]{1,0:T(8,128)(2,1)S(1)}, bf16[512,256]{1,0:T(8,128)(2,1)}, u32[]{:S(2)}) copy-start(bf16[512,256]{1,0:T(8,128)(2,1)} %constant.28.clone.refs_1_) | copy-start | bytes 786436
  36.0 13.8 %copy-start.4 = (bf16[512,256]{1,0:T(8,128)(2,1)S(1)}, bf16[512,256]{1,0:T(8,128)(2,1)}, u32[]{:S(2)}) copy-start(bf16[512,256]{1,0:T(8,128)(2,1)} %constant.32.clone.refs_2_) | copy-start | bytes 786436
  36.0 13.8 %copy-start.5 = (bf16[256,512]{1,0:T(8,128)(2,1)S(1)}, bf16[256,512]{1,0:T(8,128)(2,1)}, u32[]{:S(2)}) copy-start(bf16[256,512]{1,0:T(8,128)(2,1)} %constant.33.clone.refs_4_) | copy-start | bytes 786436
  51.1 25.5 %copy-start.9 = (f32[256]{0:T(256)S(1)}, f32[256]{0:T(256)}, u32[]{:S(2)}) copy-start(f32[256]{0:T(256)} %param.15) | copy-start | bytes 3076
  51.1 25.5 %copy-start.1 = (bf16[256,256]{1,0:T(8,128)(2,1)S(1)}, bf16[256,256]{1,0:T(8,128)(2,1)}, u32[]{:S(2)}) copy-start(bf16[256,256]{1,0:T(8,128)(2,1)} %refs_1_.2) | copy-start | bytes 393220
  51.1 25.5 %copy-start.2 = (bf16[256,256]{1,0:T(8,128)(2,1)S(1)}, bf16[256,256]{1,0:T(8,128)(2,1)}, u32[]{:S(2)}) copy-start(bf16[256,256]{1,0:T(8,128)(2,1)} %refs_2_.3) | copy-start | bytes 393220
  51.1 25.5 %copy-start.3 = (bf16[256,256]{1,0:T(8,128)(2,1)S(1)}, bf16[256,256]{1,0:T(8,128)(2,1)}, u32[]{:S(2)}) copy-start(bf16[256,256]{1,0:T(8,128)(2,1)} %refs_3_.3) | copy-start | bytes 393220

commit v8 on v7

--- a/solution.py
+++ b/solution.py
@@ -15,7 +15,7 @@
 WIDTH = 256
 LENGTH = BLOCKS * WIDTH
 SHARDS = 16
-ORDER = tuple(HALF * x + z for z in (8, 9, 10, 15, 11, 14, 12, 7, 6, 13, 4, 5, 3, 2, 1, 0) for x in (0, 1))
+ORDER = tuple(HALF * x + z for z in (8, 9, 10, 11, 15, 14, 12, 7, 6, 13, 5, 4, 3, 2, 1, 0) for x in (1, 0))
 MP_ORDER = tuple(range(SHARDS))[::-1]
 LATER = sum(1 << device for device in ORDER[HALF:])
 FACTOR = 1.0 / math.sqrt(LENGTH)

time: 78 us -> 77.4 us (level)
  no operation moved by 1% of the time
where the time goes in v8:
time: 77.4 us; the launch traced here: 77.1 us
  blocking collectives  71.2 us (92%)
  Pallas kernels  4.98 us (6%)
    all_to_all x3, blocking collectives, swap(): lax.all_to_all(block, axis, split_axis=0, concat_axis=0, tiled=True, axis...  71.2 us
    pallas_call x4, Pallas kernels, call(): pl.pallas_call(kernel, out_shape=outs[0] if single else outs, in_specs=[s...  4.98 us

profile of v8, /device:TPU:1, one launch (start us, length us, event | category | flops | bytes accessed | tf_op | source)
XLA Modules:
  0.0 77.1 jit_solution(6344440985079673440)
XLA Ops:
  0.6 0.0 copy-start
  0.7 0.0 copy-start.8
  0.7 1.5 %shard_map.130 = bf16[32,2,2176]{2,1,0:T(2,128)(2,1)S(1)} custom-call(s32[1]{0:T(128)} %bitcast.place, bf16[256,256]{1,0:T(8,128)(2,1)} %refs_1_.2, bf16[256,256]{1,0:T(8,128)(2,1)} %refs_2_.3, bf16[256,256]{1,0:T(8,128)(2,1)} %refs_3_.3, bf16[16,256]{1,0:T(8,128)(2,1)} %bitcast.3), custom_call_target="tpu_custom_call" | custom-call | flops 67108864 | bytes 679940 | tf_op jit(solution)/shard_map/pallas_call | solution.py:219
  2.2 0.0 copy-start.6
  2.2 0.0 copy-start.7
  2.2 32.4 %all_to_all.15.refs_0_ = bf16[32,2,2176]{2,1,0:T(2,128)(2,1)S(1)} all-to-all(bf16[32,2,2176]{2,1,0:T(2,128)(2,1)S(1)} %shard_map.130), channel_id=1, replica_groups={{384,128,400,144,416,160,432,176,496,240,480,224,448,192,368,112,352,96..., dimensions={0} | all-to-all | bytes 557056 | tf_op jit(solution)/shard_map/all_to_all | solution.py:231
  34.6 0.0 copy-done
  34.6 0.0 copy-done.8
  34.6 0.0 copy-done.6
  34.6 0.0 copy-done.7
  34.7 1.2 %shard_map.131 = (f32[256,512]{1,0:T(8,128)S(1)}, f32[256,512]{1,0:T(8,128)S(1)}, bf16[32,256]{1,0:T(8,128)(2,1)S(1)}, bf16[16,32,256]{2,1,0:T(8,128)(2,1)S(1)}) custom-call(s32[1]{0:T(128)} %bitcast.place, bf16[32,2,2176]{2,1,0:T(2,128)(2,1)S(1)} %all_to_all.15.refs_0_, bf16[512,256]{1,0:T(8,128)(2,1)S(1)} %copy-done.7, bf16[512,512]{1,0:T(8,128)(2,1)S(1)} %copy-done, ...), custom_call_target="tpu_custom_call" | custom-call | flops 603979776 | bytes 2719748 | tf_op jit(solution)/shard_map/pallas_call | solution.py:219
  35.8 0.0 copy-start.4
  35.8 0.0 copy-start.5
  35.8 13.6 %all_to_all.16.arrived = bf16[16,32,256]{2,1,0:T(8,128)(2,1)S(1)} all-to-all(bf16[16,32,256]{2,1,0:T(8,128)(2,1)S(1)} %get-tuple-element.10), channel_id=1, replica_groups={{15,14,13,12,11,10,9,8,7,6,5,4,3,2,1,0},{31,30,29,28,27,26,25,24,23,22,..., dimensions={0} | all-to-all | bytes 524288 | tf_op jit(solution)/shard_map/all_to_all | solution.py:231
  49.4 0.0 copy-done.4
  49.4 0.0 copy-done.5
  49.4 1.2 %shard_map.132 = bf16[32,2,2176]{2,1,0:T(2,128)(2,1)S(1)} custom-call(s32[1]{0:T(128)} %bitcast.place, bf16[16,32,256]{2,1,0:T(8,128)(2,1)S(1)} %all_to_all.16.arrived, bf16[32,256]{1,0:T(8,128)(2,1)S(1)} %get-tuple-element.11.own, f32[256,512]{1,0:T(8,128)S(1)} %get-tuple-element.12.refs_0_, f32[256,512]{1,0:T(8,128)S(1)} %get-tuple-element.13.refs_1_, ...), custom_call_target="tpu_custom_call" | custom-call | flops 603979776 | bytes 2719748 | tf_op jit(solution)/shard_map/pallas_call | solution.py:219
  50.7 0.0 copy-start.9
  50.7 0.0 copy-start.1
  50.7 0.0 copy-start.2
  50.7 0.0 copy-start.3
  50.7 25.2 %all_to_all.17.refs_0_ = bf16[32,2,2176]{2,1,0:T(2,128)(2,1)S(1)} all-to-all(bf16[32,2,2176]{2,1,0:T(2,128)(2,1)S(1)} %shard_map.132), channel_id=1, replica_groups={{384,128,400,144,416,160,432,176,496,240,480,224,448,192,368,112,352,96..., dimensions={0} | all-to-all | bytes 557056 | tf_op jit(solution)/shard_map/all_to_all | solution.py:231
  75.9 0.0 copy-done.9
  76.0 1.1 %shard_map.133 = (bf16[256,256]{1,0:T(8,128)(2,1)}, bf16[256,256]{1,0:T(8,128)(2,1)}, bf16[16,256]{1,0:T(8,128)(2,1)}) custom-call(s32[1]{0:T(128)} %bitcast.place, bf16[32,2,2176]{2,1,0:T(2,128)(2,1)S(1)} %all_to_all.17.refs_0_, bf16[256,256]{1,0:T(8,128)(2,1)S(1)} %copy-done.1, bf16[256,256]{1,0:T(8,128)(2,1)S(1)} %copy-done.2, ...), custom_call_target="tpu_custom_call" | custom-call | flops 67108864 | bytes 950276 | tf_op jit(solution)/shard_map/pallas_call | solution.py:219
  (4 shorter events, 0.0 us)
Async XLA Ops:
  0.6 34.0 %copy-start = (bf16[512,512]{1,0:T(8,128)(2,1)S(1)}, bf16[512,512]{1,0:T(8,128)(2,1)}, u32[]{:S(2)}) copy-start(bf16[512,512]{1,0:T(8,128)(2,1)} %constant.29.clone.refs_2_.refs_3_) | copy-start | bytes 1572868
  0.7 34.0 %copy-start.8 = (bf16[256,512]{1,0:T(8,128)(2,1)S(1)}, bf16[256,512]{1,0:T(8,128)(2,1)}, u32[]{:S(2)}) copy-start(bf16[256,512]{1,0:T(8,128)(2,1)} %constant.30.clone.refs_3_) | copy-start | bytes 786436
  2.2 32.5 %copy-start.6 = (f32[2,32,256]{2,1,0:T(8,128)S(1)}, f32[2,32,256]{2,1,0:T(8,128)}, u32[]{:S(2)}) copy-start(f32[2,32,256]{2,1,0:T(8,128)} %constant.31.clone.refs_4_.refs_5_) | copy-start | bytes 196612
  2.2 32.5 %copy-start.7 = (bf16[512,256]{1,0:T(8,128)(2,1)S(1)}, bf16[512,256]{1,0:T(8,128)(2,1)}, u32[]{:S(2)}) copy-start(bf16[512,256]{1,0:T(8,128)(2,1)} %constant.28.clone.refs_1_) | copy-start | bytes 786436
  35.8 13.6 %copy-start.4 = (bf16[512,256]{1,0:T(8,128)(2,1)S(1)}, bf16[512,256]{1,0:T(8,128)(2,1)}, u32[]{:S(2)}) copy-start(bf16[512,256]{1,0:T(8,128)(2,1)} %constant.32.clone.refs_2_) | copy-start | bytes 786436
  35.8 13.6 %copy-start.5 = (bf16[256,512]{1,0:T(8,128)(2,1)S(1)}, bf16[256,512]{1,0:T(8,128)(2,1)}, u32[]{:S(2)}) copy-start(bf16[256,512]{1,0:T(8,128)(2,1)} %constant.33.clone.refs_4_) | copy-start | bytes 786436
  50.7 25.3 %copy-start.9 = (f32[256]{0:T(256)S(1)}, f32[256]{0:T(256)}, u32[]{:S(2)}) copy-start(f32[256]{0:T(256)} %param.15) | copy-start | bytes 3076
  50.7 25.3 %copy-start.1 = (bf16[256,256]{1,0:T(8,128)(2,1)S(1)}, bf16[256,256]{1,0:T(8,128)(2,1)}, u32[]{:S(2)}) copy-start(bf16[256,256]{1,0:T(8,128)(2,1)} %refs_1_.2) | copy-start | bytes 393220
  50.7 25.3 %copy-start.2 = (bf16[256,256]{1,0:T(8,128)(2,1)S(1)}, bf16[256,256]{1,0:T(8,128)(2,1)}, u32[]{:S(2)}) copy-start(bf16[256,256]{1,0:T(8,128)(2,1)} %refs_2_.3) | copy-start | bytes 393220
  50.7 25.3 %copy-start.3 = (bf16[256,256]{1,0:T(8,128)(2,1)S(1)}, bf16[256,256]{1,0:T(8,128)(2,1)}, u32[]{:S(2)}) copy-start(bf16[256,256]{1,0:T(8,128)(2,1)} %refs_3_.3) | copy-start | bytes 393220

commit v9 on v8

--- a/solution.py
+++ b/solution.py
@@ -16,7 +16,7 @@
 LENGTH = BLOCKS * WIDTH
 SHARDS = 16
 ORDER = tuple(HALF * x + z for z in (8, 9, 10, 11, 15, 14, 12, 7, 6, 13, 5, 4, 3, 2, 1, 0) for x in (1, 0))
-MP_ORDER = tuple(range(SHARDS))[::-1]
+MP_ORDER = (14, 10, 6, 2, 12, 8, 4, 0, 15, 11, 7, 3, 13, 9, 5, 1)
 LATER = sum(1 << device for device in ORDER[HALF:])
 FACTOR = 1.0 / math.sqrt(LENGTH)
 VMEM = 32 * 1024 * 1024
@@ -55,7 +55,11 @@
 
 
 def shard_at(place):
-    return SHARDS - 1 - place
+    return 14 - 4 * (place & 3) - 2 * (place >> 2 & 1) + (place >> 3)
+
+
+def place_of(shard):
+    return 8 * (shard & 1) + 4 * (1 - (shard >> 1 & 1)) + 3 - (shard >> 2)
 
 
 def source_of(half, row, place):
@@ -236,7 +240,7 @@
     spectrum = jax.ShapeDtypeStruct((WIDTH, 2 * WIDTH), jnp.float32)
     packed = shape((BLOCKS, 2, 8 * WIDTH + 128))
     later = lax.shift_right_logical(np.uint32(LATER), lax.axis_index("ctx").astype(jnp.uint32)) & 1
-    place = (later.astype(jnp.int32) * SHARDS + shard_at(lax.axis_index("mp"))).reshape(1)
+    place = (later.astype(jnp.int32) * SHARDS + place_of(lax.axis_index("mp"))).reshape(1)
     skip_rows = jnp.broadcast_to(skip_gain[None, :], (8, WIDTH))
     cube = 2 * WIDTH**3
 

time: 77.4 us -> 77.4 us (level)
  no operation moved by 1% of the time
where the time goes in v9:
time: 77.4 us; the launch traced here: 76.5 us
  blocking collectives  70.7 us (91%)
  Pallas kernels  5.02 us (6%)
    all_to_all x3, blocking collectives, swap(): lax.all_to_all(block, axis, split_axis=0, concat_axis=0, tiled=True, axis...  70.7 us
    pallas_call x4, Pallas kernels, call(): pl.pallas_call(kernel, out_shape=outs[0] if single else outs, in_specs=[s...  5.02 us

profile of v9, /device:TPU:1, one launch (start us, length us, event | category | flops | bytes accessed | tf_op | source)
XLA Modules:
  0.0 76.5 jit_solution(8500917430739661529)
XLA Ops:
  0.6 0.0 copy-start
  0.7 0.0 copy-start.8
  0.7 1.5 %shard_map.130 = bf16[32,2,2176]{2,1,0:T(2,128)(2,1)S(1)} custom-call(s32[1]{0:T(128)} %bitcast.place, bf16[256,256]{1,0:T(8,128)(2,1)} %refs_1_.2, bf16[256,256]{1,0:T(8,128)(2,1)} %refs_2_.3, bf16[256,256]{1,0:T(8,128)(2,1)} %refs_3_.3, bf16[16,256]{1,0:T(8,128)(2,1)} %bitcast.3), custom_call_target="tpu_custom_call" | custom-call | flops 67108864 | bytes 679940 | tf_op jit(solution)/shard_map/pallas_call | solution.py:223
  2.2 0.0 copy-start.6
  2.2 0.0 copy-start.7
  2.2 32.4 %all_to_all.15.refs_0_ = bf16[32,2,2176]{2,1,0:T(2,128)(2,1)S(1)} all-to-all(bf16[32,2,2176]{2,1,0:T(2,128)(2,1)S(1)} %shard_map.130), channel_id=1, replica_groups={{384,128,400,144,416,160,432,176,496,240,480,224,448,192,368,112,352,96..., dimensions={0} | all-to-all | bytes 557056 | tf_op jit(solution)/shard_map/all_to_all | solution.py:235
  34.6 0.0 copy-done
  34.6 0.0 copy-done.8
  34.6 0.0 copy-done.6
  34.6 0.0 copy-done.7
  34.7 1.2 %shard_map.131 = (f32[256,512]{1,0:T(8,128)S(1)}, f32[256,512]{1,0:T(8,128)S(1)}, bf16[32,256]{1,0:T(8,128)(2,1)S(1)}, bf16[16,32,256]{2,1,0:T(8,128)(2,1)S(1)}) custom-call(s32[1]{0:T(128)} %bitcast.place, bf16[32,2,2176]{2,1,0:T(2,128)(2,1)S(1)} %all_to_all.15.refs_0_, bf16[512,256]{1,0:T(8,128)(2,1)S(1)} %copy-done.7, bf16[512,512]{1,0:T(8,128)(2,1)S(1)} %copy-done, ...), custom_call_target="tpu_custom_call" | custom-call | flops 603979776 | bytes 2719748 | tf_op jit(solution)/shard_map/pallas_call | solution.py:223
  35.8 0.0 copy-start.4
  35.8 0.0 copy-start.5
  35.8 14.0 %all_to_all.16.arrived = bf16[16,32,256]{2,1,0:T(8,128)(2,1)S(1)} all-to-all(bf16[16,32,256]{2,1,0:T(8,128)(2,1)S(1)} %get-tuple-element.10), channel_id=1, replica_groups={{14,10,6,2,12,8,4,0,15,11,7,3,13,9,5,1},{30,26,22,18,28,24,20,16,31,27,..., dimensions={0} | all-to-all | bytes 524288 | tf_op jit(solution)/shard_map/all_to_all | solution.py:235
  49.8 0.0 copy-done.4
  49.8 1.2 %shard_map.132 = bf16[32,2,2176]{2,1,0:T(2,128)(2,1)S(1)} custom-call(s32[1]{0:T(128)} %bitcast.place, bf16[16,32,256]{2,1,0:T(8,128)(2,1)S(1)} %all_to_all.16.arrived, bf16[32,256]{1,0:T(8,128)(2,1)S(1)} %get-tuple-element.11.own, f32[256,512]{1,0:T(8,128)S(1)} %get-tuple-element.12.refs_0_, f32[256,512]{1,0:T(8,128)S(1)} %get-tuple-element.13.refs_1_, ...), custom_call_target="tpu_custom_call" | custom-call | flops 603979776 | bytes 2719748 | tf_op jit(solution)/shard_map/pallas_call | solution.py:223
  51.1 0.0 copy-start.9
  51.1 0.0 copy-start.1
  51.1 0.0 copy-start.2
  51.1 0.0 copy-start.3
  51.1 24.3 %all_to_all.17.refs_0_ = bf16[32,2,2176]{2,1,0:T(2,128)(2,1)S(1)} all-to-all(bf16[32,2,2176]{2,1,0:T(2,128)(2,1)S(1)} %shard_map.132), channel_id=1, replica_groups={{384,128,400,144,416,160,432,176,496,240,480,224,448,192,368,112,352,96..., dimensions={0} | all-to-all | bytes 557056 | tf_op jit(solution)/shard_map/all_to_all | solution.py:235
  75.4 0.0 copy-done.1
  75.4 0.0 copy-done.3
  75.4 1.1 %shard_map.133 = (bf16[256,256]{1,0:T(8,128)(2,1)}, bf16[256,256]{1,0:T(8,128)(2,1)}, bf16[16,256]{1,0:T(8,128)(2,1)}) custom-call(s32[1]{0:T(128)} %bitcast.place, bf16[32,2,2176]{2,1,0:T(2,128)(2,1)S(1)} %all_to_all.17.refs_0_, bf16[256,256]{1,0:T(8,128)(2,1)S(1)} %copy-done.1, bf16[256,256]{1,0:T(8,128)(2,1)S(1)} %copy-done.2, ...), custom_call_target="tpu_custom_call" | custom-call | flops 67108864 | bytes 950276 | tf_op jit(solution)/shard_map/pallas_call | solution.py:223
  (4 shorter events, 0.0 us)
Async XLA Ops:
  0.6 34.0 %copy-start = (bf16[512,512]{1,0:T(8,128)(2,1)S(1)}, bf16[512,512]{1,0:T(8,128)(2,1)}, u32[]{:S(2)}) copy-start(bf16[512,512]{1,0:T(8,128)(2,1)} %constant.37.clone.refs_2_.refs_3_) | copy-start | bytes 1572868
  0.7 34.0 %copy-start.8 = (bf16[256,512]{1,0:T(8,128)(2,1)S(1)}, bf16[256,512]{1,0:T(8,128)(2,1)}, u32[]{:S(2)}) copy-start(bf16[256,512]{1,0:T(8,128)(2,1)} %constant.38.clone.refs_3_) | copy-start | bytes 786436
  2.2 32.5 %copy-start.6 = (f32[2,32,256]{2,1,0:T(8,128)S(1)}, f32[2,32,256]{2,1,0:T(8,128)}, u32[]{:S(2)}) copy-start(f32[2,32,256]{2,1,0:T(8,128)} %constant.39.clone.refs_4_.refs_5_) | copy-start | bytes 196612
  2.2 32.5 %copy-start.7 = (bf16[512,256]{1,0:T(8,128)(2,1)S(1)}, bf16[512,256]{1,0:T(8,128)(2,1)}, u32[]{:S(2)}) copy-start(bf16[512,256]{1,0:T(8,128)(2,1)} %constant.36.clone.refs_1_) | copy-start | bytes 786436
  35.8 14.0 %copy-start.4 = (bf16[512,256]{1,0:T(8,128)(2,1)S(1)}, bf16[512,256]{1,0:T(8,128)(2,1)}, u32[]{:S(2)}) copy-start(bf16[512,256]{1,0:T(8,128)(2,1)} %constant.40.clone.refs_2_) | copy-start | bytes 786436
  35.8 14.0 %copy-start.5 = (bf16[256,512]{1,0:T(8,128)(2,1)S(1)}, bf16[256,512]{1,0:T(8,128)(2,1)}, u32[]{:S(2)}) copy-start(bf16[256,512]{1,0:T(8,128)(2,1)} %constant.41.clone.refs_4_) | copy-start | bytes 786436
  51.1 24.3 %copy-start.9 = (f32[256]{0:T(256)S(1)}, f32[256]{0:T(256)}, u32[]{:S(2)}) copy-start(f32[256]{0:T(256)} %param.15) | copy-start | bytes 3076
  51.1 24.3 %copy-start.1 = (bf16[256,256]{1,0:T(8,128)(2,1)S(1)}, bf16[256,256]{1,0:T(8,128)(2,1)}, u32[]{:S(2)}) copy-start(bf16[256,256]{1,0:T(8,128)(2,1)} %refs_1_.2) | copy-start | bytes 393220
  51.1 24.3 %copy-start.2 = (bf16[256,256]{1,0:T(8,128)(2,1)S(1)}, bf16[256,256]{1,0:T(8,128)(2,1)}, u32[]{:S(2)}) copy-start(bf16[256,256]{1,0:T(8,128)(2,1)} %refs_2_.3) | copy-start | bytes 393220
  51.1 24.3 %copy-start.3 = (bf16[256,256]{1,0:T(8,128)(2,1)S(1)}, bf16[256,256]{1,0:T(8,128)(2,1)}, u32[]{:S(2)}) copy-start(bf16[256,256]{1,0:T(8,128)(2,1)} %refs_3_.3) | copy-start | bytes 393220
